TPU v7x, 32 devices: a whole 2x2x4 slice. The times are simulated.
32 devices in a mesh: wide: 8 (over z, y), narrow: 4 (over x, core).
Axes of the slice: x: 2, y: 2, z: 4, core: 2. Of those that a mesh axis runs over, the one named last changes fastest.
Arguments:
- state: bfloat16 [1024, 1024, 128], P(('wide', 'narrow')), may hold values from -6 to 6
- group_of: int32 [1024], replicated, may hold values from 0 to 1023, as said below
- w_in: bfloat16 [1024, 1024], replicated, may hold values from -0.1875 to 0.1875
- w_out: bfloat16 [1024, 1024], replicated, may hold values from -0.1875 to 0.1875
- w_flux: bfloat16 [32, 1024], replicated, may hold values from -0.1875 to 0.1875
- owner: int32 [131072, 1], P(('wide', 'narrow')), may hold values from 0 to 31; in each aligned block of 4096 rows (0 to 4095, 4096 to 8191, ...) at most 256 rows name the same one
- ocean_slot: int32 [131072], P(('wide', 'narrow')), may hold values from 0 to 511
- remap_weight: float32 [131072], P(('wide', 'narrow')), may hold values from 0.25 to 4
Outputs:
- new_state: bfloat16 [1024, 1024, 128], P(('wide', 'narrow'))
- ocean: float32 [32, 16384], P(None, ('wide', 'narrow'))
Inputs may be any that keep to these rules, and one draw needn't show every extreme that they name: group_of is a permutation of the blocks. Block p = ((w * 4 + n) * 32 + s) keeps n and s; for each n exactly 4 slots s move, each to wide index (w + c) modulo the wide size with a nonzero c of its own, and all other blocks stay.
All inputs are finite; a program needn't handle non-finite values.
Results may differ from a plain program's by a relative error of at most 0.0044.
Values may be sent and summed in bfloat16 or wider, within the bound.
No kernel may reach another device: no remote copies, remote signals or barrier semaphores. Data moves between devices by JAX's collectives and lax.ppermute only.
A program may use at most 192 MiB of HBM per device.

v0:
```python
import functools

import jax
import jax.numpy as jnp
from jax import lax
from jax.experimental import pallas as pl
from jax.experimental.pallas import tpu as pltpu
from jax.sharding import PartitionSpec as P

OCN_DEV = 512
LANES = 256
GROUP = 4
STEP = 256
MIB = 1024 * 1024


def silu(v):
    u = 0.5 * v
    return u + u * jnp.tanh(u)


def side_by_side(blocks):
    return jnp.concatenate([blocks[j] for j in range(GROUP)], axis=1)


def hidden_of(x, w_in, hid, loads=()):
    for i, r in enumerate(range(0, w_in.shape[0], STEP)):
        if loads and i > 0:
            loads[i].wait()
        v = jnp.dot(w_in[r : r + STEP, :], x, preferred_element_type=jnp.float32)
        hid[r : r + STEP, :] = silu(v).astype(jnp.bfloat16)


def updated(buf_in, hid, w_out, buf_out, loads=()):
    cols = buf_in.shape[2]
    h = hid[...]
    for i, r in enumerate(range(0, w_out.shape[0], STEP)):
        if loads:
            loads[i].wait()
        t = jnp.dot(w_out[r : r + STEP, :], h, preferred_element_type=jnp.float32)
        for j in range(GROUP):
            old = buf_in[j, r : r + STEP, :].astype(jnp.float32)
            buf_out[j, r : r + STEP, :] = (old + t[:, j * cols : (j + 1) * cols]).astype(jnp.bfloat16)


def block_copies(hbm, row_of, vmem, sem, g, b, into_vmem):
    copies = []
    for j in range(GROUP):
        there = hbm.at[row_of(g * GROUP + j)]
        src, dst = (there, vmem.at[b, j]) if into_vmem else (vmem.at[b, j], there)
        copies.append(pltpu.make_async_copy(src, dst, sem.at[b, j]))
    return copies


def start(copies):
    for c in copies:
        c.start()


def wait(copies):
    for c in copies:
        c.wait()


def order_kernel(
    nwide, nnarrow, move, table_hbm, owner_hbm, slot_hbm, weight_hbm, order, meta_hbm,
    table, owner, slot, weight, meta, sem,
):
    blocks = owner.shape[0]
    stay = blocks - move
    pairs = [(table_hbm, table), (owner_hbm, owner), (slot_hbm, slot), (weight_hbm, weight)]
    loads = [pltpu.make_async_copy(src, dst, sem.at[i]) for i, (src, dst) in enumerate(pairs)]
    start(loads)
    me = lax.axis_index("wide")
    base = (me * nnarrow + lax.axis_index("narrow")) * blocks
    loads[0].wait()

    def look(s, counts):
        kept, gone = counts
        dest = lax.div(table[base + s], nnarrow * blocks)
        leaves = dest != me
        order[jnp.where(leaves, stay + gone, kept)] = s
        order[blocks + s] = dest
        order[2 * blocks + s] = lax.rem(2 * me - dest + nwide, nwide)
        step = leaves.astype(jnp.int32)
        return kept + 1 - step, gone + step

    lax.fori_loop(0, blocks, look, (jnp.int32(0), jnp.int32(0)))
    wait(loads[1:])
    meta[...] = jnp.zeros_like(meta)
    for k in range(move):
        s = order[stay + k]
        source = order[2 * blocks + s]
        cell = owner[pl.ds(s, 1), :] * OCN_DEV + slot[pl.ds(s, 1), :]
        meta[source, 0:1, :] = cell.astype(jnp.float32)
        meta[source, 1:2, :] = weight[pl.ds(s, 1), :]
    save = pltpu.make_async_copy(meta, meta_hbm, sem.at[len(pairs)])
    save.start()
    save.wait()


def row_parts(src, dst, sem):
    parts = []
    for i, r in enumerate(range(0, src.shape[0], STEP)):
        rows = pl.ds(r, STEP)
        parts.append(pltpu.make_async_copy(src.at[rows], dst.at[rows], sem.at[i]))
    return parts


def leaving_kernel(
    order, state, w_in_hbm, w_out_hbm, w_flux_hbm, out, flux,
    w_in, w_out, w_flux, buf_in, buf_out, hid, sem_w, sem_f, sem_in, sem_out,
):
    blocks, _, cols = state.shape
    move = flux.shape[0]
    stay = blocks - move

    def slot_of(k):
        return order[stay + k]

    def row_of(k):
        return order[blocks + order[stay + k]]

    groups = move // GROUP
    start(block_copies(state, slot_of, buf_in, sem_in, 0, 0, True))
    load_in = row_parts(w_in_hbm, w_in, sem_w.at[0])
    load_out = row_parts(w_out_hbm, w_out, sem_w.at[1])
    load_flux = pltpu.make_async_copy(w_flux_hbm, w_flux, sem_f)
    start(load_in)
    for g in range(groups):
        b = g % 2
        wait(block_copies(state, slot_of, buf_in, sem_in, g, b, True))
        if g == 0:
            load_in[0].wait()
            start(load_out)
            load_flux.start()
        if g + 1 < groups:
            start(block_copies(state, slot_of, buf_in, sem_in, g + 1, 1 - b, True))
        if g >= 2:
            wait(block_copies(out, row_of, buf_out, sem_out, g - 2, b, False))
        hidden_of(side_by_side(buf_in.at[b]), w_in, hid, load_in if g == 0 else ())
        updated(buf_in.at[b], hid, w_out, buf_out.at[b], load_out if g == 0 else ())
        start(block_copies(out, row_of, buf_out, sem_out, g, b, False))
        if g == 0:
            load_flux.wait()
        f = jnp.dot(w_flux[...], hid[...], preferred_element_type=jnp.float32)
        for j in range(GROUP):
            flux[g * GROUP + j] = f[:, j * cols : (j + 1) * cols]
    for g in range(max(groups - 2, 0), groups):
        wait(block_copies(out, row_of, buf_out, sem_out, g, g % 2, False))


def hidden_kernel(
    order, state, w_in_hbm, w_out_hbm, w_flux_hbm, hidden, flux, kept, w_out,
    w_in, w_flux, sem_w, sem_f, sem_kept,
):
    groups, _, _, cols = kept.shape

    def arrivals(g):
        return [
            pltpu.make_async_copy(state.at[order[g * GROUP + j]], kept.at[g, j], sem_kept.at[g, j])
            for j in range(GROUP)
        ]

    load_in = row_parts(w_in_hbm, w_in, sem_w.at[0])
    load_out = row_parts(w_out_hbm, w_out, sem_w.at[1])
    load_flux = pltpu.make_async_copy(w_flux_hbm, w_flux, sem_f)
    start(arrivals(0))
    start(load_in)
    load_flux.start()

    def work(g, loads):
        hidden_of(side_by_side(kept.at[g]), w_in, hidden.at[g], loads)
        if loads:
            load_flux.wait()
        f = jnp.dot(w_flux[...], hidden[g], preferred_element_type=jnp.float32)
        for j in range(GROUP):
            flux[g * GROUP + j] = f[:, j * cols : (j + 1) * cols]

    wait(arrivals(0))
    load_in[0].wait()
    if groups > 1:
        start(arrivals(1))
    work(0, load_in)

    @pl.loop(1, groups)
    def _(g):
        wait(arrivals(g))

        @pl.when(g + 1 < groups)
        def _():
            start(arrivals(g + 1))

        @pl.when(g + 1 == groups)
        def _():
            start(load_out)

        work(g, ())

    if groups == 1:
        start(load_out)
    wait(load_out)


def update_kernel(first, last, order, kept, hidden, w_out, *rest):
    out, buf_out, sem_out = rest[-3:]

    def departures(g):
        return block_copies(out, lambda k: order[k], buf_out, sem_out, g, g - first, False)

    @pl.loop(first, last)
    def _(g):
        updated(kept.at[g], hidden.at[g], w_out, buf_out.at[g - first])
        start(departures(g))

    for g in range(first, last):
        wait(departures(g))


def fill(devices, device, j, f, cell, area, left, right):
    nflux, cols = f.shape
    halves = OCN_DEV // LANES
    bf16 = jnp.bfloat16
    bits = devices.bit_length() - 1
    f = (f * area).astype(bf16)
    apart = (cell // OCN_DEV) ^ device
    far = jnp.zeros_like(apart)
    for i in range(bits):
        far = far | (((apart >> i) & 1) << (bits - 1 - i))
    high = far * halves + (cell % OCN_DEV) // LANES
    low = cell % LANES
    high = jnp.broadcast_to(high.astype(jnp.float32), (nflux, cols)).astype(bf16)
    low = jnp.broadcast_to(low.astype(jnp.float32), (LANES, cols)).astype(bf16)
    rows = lax.broadcasted_iota(jnp.int32, (LANES, cols), 0).astype(jnp.float32).astype(bf16)
    one, zero = jnp.ones((), bf16), jnp.zeros((), bf16)
    right[:, j * cols : (j + 1) * cols] = jnp.where(low == rows, one, zero)
    for h in range(devices * halves):
        left[h * nflux : (h + 1) * nflux, j * cols : (j + 1) * cols] = jnp.where(
            high == jnp.asarray(h, bf16), f, zero
        )


def product(left, right):
    return lax.dot_general(
        left[...], right[...], (((1,), (1,)), ((), ())), preferred_element_type=jnp.float32
    )


def device_index(nnarrow):
    return lax.axis_index("wide") * nnarrow + lax.axis_index("narrow")


def cells_kernel(
    devices, nnarrow, order, flux, flux_away, meta, owner, slot, weight, keep, send, left, right, total
):
    stay, move = flux.shape[0], flux_away.shape[0]
    blocks = stay + move
    device = device_index(nnarrow)
    half = total.shape[0] // 2
    total[...] = jnp.zeros_like(total)

    @pl.loop(0, stay // GROUP, unroll=stay // GROUP if devices <= 32 else 1)
    def _(g):
        b = g % left.shape[0]
        for j in range(GROUP):
            row = pl.ds(order[g * GROUP + j], 1)
            cell = owner[row, :] * OCN_DEV + slot[row, :]
            fill(devices, device, j, flux[g * GROUP + j], cell, weight[row, :], left.at[b], right.at[b])
        total[...] += product(left.at[b], right.at[b])

    for g in range(move // GROUP):
        b = g % left.shape[0]
        for j in range(GROUP):
            k = g * GROUP + j
            dest = order[blocks + order[stay + k]]
            cell = meta[dest, 0:1, :].astype(jnp.int32)
            fill(devices, device, j, flux_away[k], cell, meta[dest, 1:2, :], left.at[b], right.at[b])
        total[...] += product(left.at[b], right.at[b])
    keep[...] = total[:half, :]
    send[...] = total[half:, :].astype(jnp.bfloat16)


def halve_kernel(mine, came, keep, send):
    half = keep.shape[0]
    keep[...] = mine[:half, :] + came[:half, :].astype(jnp.float32)
    send[...] = (mine[half:, :] + came[half:, :].astype(jnp.float32)).astype(jnp.bfloat16)


def last_kernel(mine, came, out):
    nflux = out.shape[0]
    for h in range(OCN_DEV // LANES):
        rows = slice(h * nflux, (h + 1) * nflux)
        out[:, h * LANES : (h + 1) * LANES] = mine[rows, :] + came[rows, :].astype(jnp.float32)


def place_kernel(move, order, arrived, partial, out, sem):
    blocks = out.shape[0]
    stay = blocks - move
    copies = []
    for k in range(move):
        s = order[stay + k]
        copies.append(
            pltpu.make_async_copy(arrived.at[order[2 * blocks + s]], out.at[s], sem.at[k])
        )
    start(copies)
    wait(copies)


SMEM = pl.BlockSpec(memory_space=pltpu.SMEM)
VMEM = pl.BlockSpec(memory_space=pltpu.VMEM)
HBM = pl.BlockSpec(memory_space=pltpu.HBM)
ANY = pl.BlockSpec(memory_space=pl.ANY)


def per_device(state, group_of, w_in, w_out, w_flux, owner, ocean_slot, remap_weight):
    nwide = lax.axis_size("wide")
    nnarrow = lax.axis_size("narrow")
    blocks, depth, cols = state.shape
    inner = w_in.shape[0]
    nflux = w_flux.shape[0]
    devices = nwide * nnarrow
    move = nwide // 2
    stay = blocks - move
    bf16, f32, i32 = jnp.bfloat16, jnp.float32, jnp.int32
    shape = jax.ShapeDtypeStruct
    dma = pltpu.SemaphoreType.DMA
    side = GROUP * cols
    owner = owner[:, 0].reshape(blocks, cols)
    slot = ocean_slot.reshape(blocks, cols)
    weight = remap_weight.reshape(blocks, cols)
    params = pltpu.CompilerParams(vmem_limit_bytes=20 * MIB)
    buffers = 2 if devices <= 32 else 1
    in_hbm = functools.partial(pltpu.with_memory_space_constraint, memory_space=pltpu.HBM)
    in_vmem = functools.partial(pltpu.with_memory_space_constraint, memory_space=pltpu.VMEM)

    def cost(n, products):
        return pl.CostEstimate(
            flops=2 * n * cols * inner * depth * products,
            bytes_accessed=4 * n * depth * cols + 2 * inner * depth * products,
            transcendentals=n * cols * inner,
        )

    def swap(x, axis, bit):
        return lax.ppermute(x, axis, [(i, i ^ bit) for i in range(lax.axis_size(axis))])

    with jax.named_scope("order_of_blocks"):
        order, meta = pl.pallas_call(
            functools.partial(order_kernel, nwide, nnarrow, move),
            out_shape=(shape((3 * blocks,), i32), pltpu.HBM((nwide, 8, cols), f32)),
            in_specs=[HBM] * 4,
            out_specs=(SMEM, HBM),
            scratch_shapes=[
                pltpu.SMEM(group_of.shape, i32),
                pltpu.VMEM((blocks, cols), i32),
                pltpu.VMEM((blocks, cols), i32),
                pltpu.VMEM((blocks, cols), f32),
                pltpu.VMEM((nwide, 8, cols), f32),
                dma((5,)),
            ],
            compiler_params=params,
        )(in_hbm(group_of), in_hbm(owner), in_hbm(slot), in_hbm(weight))
    meta = lax.all_to_all(meta, "wide", split_axis=0, concat_axis=0, tiled=True)

    groups = stay // GROUP
    parts = max(inner, depth) // STEP
    with jax.named_scope("leaving_blocks"):
        outgoing, flux_away = pl.pallas_call(
            leaving_kernel,
            out_shape=(pltpu.HBM((nwide, depth, cols), bf16), shape((move, nflux, cols), f32)),
            in_specs=[SMEM, HBM, HBM, HBM, HBM],
            out_specs=(HBM, VMEM),
            scratch_shapes=[
                pltpu.VMEM((inner, depth), bf16),
                pltpu.VMEM((depth, inner), bf16),
                pltpu.VMEM((nflux, inner), bf16),
                pltpu.VMEM((2, GROUP, depth, cols), bf16),
                pltpu.VMEM((2, GROUP, depth, cols), bf16),
                pltpu.VMEM((inner, side), bf16),
                dma((2, parts)),
                dma,
                dma((2, GROUP)),
                dma((2, GROUP)),
            ],
            compiler_params=params,
            cost_estimate=cost(move, 2),
        )(order, in_hbm(state), in_hbm(w_in), in_hbm(w_out), in_hbm(w_flux))
    outgoing, meta = lax.optimization_barrier((outgoing, meta))
    arrived = lax.all_to_all(outgoing, "wide", split_axis=0, concat_axis=0, tiled=True)

    with jax.named_scope("hidden_of_staying_blocks"):
        hidden, flux, kept, w_out = pl.pallas_call(
            hidden_kernel,
            out_shape=(
                pltpu.VMEM((groups, inner, side), bf16),
                shape((stay, nflux, cols), f32),
                pltpu.VMEM((groups, GROUP, depth, cols), bf16),
                pltpu.VMEM(w_out.shape, bf16),
            ),
            in_specs=[SMEM, HBM, HBM, HBM, HBM],
            out_specs=(VMEM, VMEM, VMEM, VMEM),
            scratch_shapes=[
                pltpu.VMEM((inner, depth), bf16),
                pltpu.VMEM((nflux, inner), bf16),
                dma((2, parts)),
                dma,
                dma((groups, GROUP)),
            ],
            compiler_params=params,
            cost_estimate=cost(stay, 1),
        )(order, in_hbm(state), in_hbm(w_in), in_hbm(w_out), in_hbm(w_flux))

    rows = devices * nflux * OCN_DEV // LANES
    with jax.named_scope("cell_sums"):
        keep, send = pl.pallas_call(
            functools.partial(cells_kernel, devices, nnarrow),
            out_shape=(shape((rows // 2, LANES), f32), shape((rows // 2, LANES), bf16)),
            in_specs=[SMEM] + [VMEM] * 6,
            out_specs=(VMEM, VMEM),
            scratch_shapes=[
                pltpu.VMEM((buffers, rows, side), bf16),
                pltpu.VMEM((buffers, LANES, side), bf16),
                pltpu.VMEM((rows, LANES), f32),
            ],
            compiler_params=pltpu.CompilerParams(vmem_limit_bytes=16 * MIB + 16 * rows * LANES),
            cost_estimate=pl.CostEstimate(
                flops=2 * rows * LANES * blocks * cols, bytes_accessed=6 * rows * LANES, transcendentals=0
            ),
        )(order, flux, flux_away, meta, owner, slot, weight)

    steps = devices.bit_length() - 1
    partial = None
    done = 0

    def update(upto, partial, after):
        begun = () if partial is None else (partial,)
        return pl.pallas_call(
            functools.partial(update_kernel, done, upto),
            out_shape=shape(state.shape, bf16),
            in_specs=[SMEM, VMEM, VMEM, VMEM, ANY] + [ANY] * len(begun),
            out_specs=ANY,
            scratch_shapes=[
                pltpu.VMEM((upto - done, GROUP, depth, cols), bf16),
                dma((upto - done, GROUP)),
            ],
            input_output_aliases={5: 0} if begun else {},
            compiler_params=params,
            cost_estimate=cost((upto - done) * GROUP, 1),
        )(order, in_vmem(kept), in_vmem(hidden), in_vmem(w_out), after, *begun)

    with jax.named_scope("ocean_sums"):
        rows //= 2
        step = 0
        for axis, size in (("narrow", nnarrow), ("wide", nwide)):
            bit = 1
            while bit < size:
                came = swap(send, axis, bit)
                if step > 0:
                    upto = groups if step == steps - 1 else min(groups, done + -(-groups // (steps - 1)))
                    if upto > done:
                        with jax.named_scope("update_of_staying_blocks"):
                            partial = update(upto, partial, keep)
                        done = upto
                if step < steps - 1:
                    rows //= 2
                    keep, send = pl.pallas_call(
                        halve_kernel,
                        out_shape=(shape((rows, LANES), f32), shape((rows, LANES), bf16)),
                        in_specs=[VMEM, VMEM],
                        out_specs=(VMEM, VMEM),
                        compiler_params=params,
                    )(keep, came)
                else:
                    ocean = pl.pallas_call(
                        last_kernel,
                        out_shape=shape((nflux, OCN_DEV), f32),
                        in_specs=[VMEM, VMEM],
                        out_specs=VMEM,
                        compiler_params=params,
                    )(keep, came)
                bit *= 2
                step += 1

    with jax.named_scope("arrived_blocks"):
        new_state = pl.pallas_call(
            functools.partial(place_kernel, move),
            out_shape=shape(state.shape, bf16),
            in_specs=[SMEM, VMEM, ANY],
            out_specs=ANY,
            scratch_shapes=[dma((move,))],
            input_output_aliases={2: 0},
            compiler_params=params,
        )(order, arrived, partial)
    return (new_state, ocean)


def solution(mesh):
    in_specs = (
        P(("wide", "narrow"), None, None),
        P(),
        P(),
        P(),
        P(),
        P(("wide", "narrow"), None),
        P(("wide", "narrow")),
        P(("wide", "narrow")),
    )
    out_specs = (P(("wide", "narrow"), None, None), P(None, ("wide", "narrow")))
    return jax.shard_map(
        per_device, mesh=mesh, in_specs=in_specs, out_specs=out_specs, check_vma=False
    )
```

profile of v0, /device:TPU:0, one launch (start us, length us, event | category | flops | bytes accessed | tf_op | source)
XLA Modules:
  0.0 79.8 jit_solution(17510922688670407872)
XLA Ops:
  0.6 2.5 %order_of_blocks.1 = (s32[96]{0:T(128)S(1)}, f32[8,8,128]{2,1,0:T(8,128)}) custom-call(s32[1024]{0:T(1024)} %table_hbm.1, s32[32,128]{1,0:T(8,128)} %bitcast.3, s32[32,128]{1,0:T(8,128)} %bitcast.5, f32[32,128]{1,0:T(8,128)} %bitcast.7), custom_call_target="tpu_custom_call" | custom-call | tf_op jit(solution)/shard_map/order_of_blocks/pallas_call | solution.py:347
  3.1 7.3 %all-to-all-start = ((f32[8,8,128]{2,1,0:T(8,128)}), f32[8,8,128]{2,1,0:T(8,128)S(1)}, u32[]{:S(2)}, u32[]{:S(2)}) async-start(f32[8,8,128]{2,1,0:T(8,128)} %get-tuple-element.24), calls=%async_computation | async-start | bytes 65536 | tf_op jit(solution)/shard_map/all_to_all | solution.py:362
  10.4 7.1 %leaving_blocks.1 = (bf16[8,1024,128]{2,1,0:T(8,128)(2,1)}, f32[4,32,128]{2,1,0:T(8,128)S(1)}) custom-call(s32[96]{0:T(128)S(1)} %get-tuple-element.22.order, bf16[32,1024,128]{2,1,0:T(8,128)(2,1)} %state.3, bf16[1024,1024]{1,0:T(8,128)(2,1)} %w_in_hbm.3, bf16[1024,1024]{1,0:T(8,128)(2,1)} %w_out_hbm.3, bf16[32,1024]{1,0:T(8,128)(2,1)} %w_flux_hbm.3), custom_call_target="tpu_custom_call" | custom-call | flops 2147483648 | bytes 6291456 | tf_op jit(solution)/shard_map/leaving_blocks/pallas_call | solution.py:367
  17.5 0.0 all-to-all-done.meta
  17.5 6.0 %all-to-all-start.1 = ((bf16[8,1024,128]{2,1,0:T(8,128)(2,1)}), bf16[8,1024,128]{2,1,0:T(8,128)(2,1)S(1)}, u32[]{:S(2)}, u32[]{:S(2)}) async-start(bf16[8,1024,128]{2,1,0:T(8,128)(2,1)} %get-tuple-element.25), calls=%async_computation.1 | async-start | bytes 4194304 | tf_op jit(solution)/shard_map/all_to_all | solution.py:388
  23.5 0.0 copy-start
  23.5 0.0 copy-start.1
  23.5 0.0 copy-start.2
  23.5 14.0 %hidden_of_staying_blocks.1 = (bf16[7,1024,512]{2,1,0:T(8,128)(2,1)S(1)}, f32[28,32,128]{2,1,0:T(8,128)S(1)}, bf16[7,4,1024,128]{3,2,1,0:T(8,128)(2,1)S(1)}, bf16[1024,1024]{1,0:T(8,128)(2,1)S(1)}) custom-call(s32[96]{0:T(128)S(1)} %get-tuple-element.22.order, bf16[32,1024,128]{2,1,0:T(8,128)(2,1)} %state.3, bf16[1024,1024]{1,0:T(8,128)(2,1)} %w_in_hbm.3, ...), custom_call_target="tpu_custom_call" | custom-call | flops 7516192768 | bytes 16777216 | tf_op jit(solution)/shard_map/hidden_of_staying_blocks/pallas_call | solution.py:391
  37.5 0.0 copy-done
  37.5 0.0 copy-done.1
  37.6 0.0 copy-done.2
  37.6 7.4 %cell_sums.1 = (f32[1024,256]{1,0:T(8,128)S(1)}, bf16[1024,256]{1,0:T(8,128)(2,1)S(1)}) custom-call(s32[96]{0:T(128)S(1)} %get-tuple-element.22.order, f32[28,32,128]{2,1,0:T(8,128)S(1)} %get-tuple-element.29.flux, f32[4,32,128]{2,1,0:T(8,128)S(1)} %get-tuple-element.30.flux_away, f32[8,8,128]{2,1,0:T(8,128)S(1)} %all-to-all-done.meta, ...), custom_call_target="tpu_custom_call" | custom-call | flops 4294967296 | bytes 3145728 | tf_op jit(solution)/shard_map/cell_sums/pallas_call | solution.py:414
  45.0 0.1 collective-permute-start
  45.1 1.9 %collective-permute-done.came = bf16[1024,256]{1,0:T(8,128)(2,1)S(1)} collective-permute-done((bf16[1024,256]{1,0:T(8,128)(2,1)S(1)}, bf16[1024,256]{1,0:T(8,128)(2,1)S(1)}, u32[]{:S(2)}, u32[]{:S(2)}) %collective-permute-start) | collective-permute-done | bytes 524320 | tf_op jit(solution)/shard_map/ocean_sums/ppermute | solution.py:344
  47.0 0.1 ocean_sums.5
  47.1 1.6 %collective-permute-start.1 = (bf16[512,256]{1,0:T(8,128)(2,1)S(1)}, bf16[512,256]{1,0:T(8,128)(2,1)S(1)}, u32[]{:S(2)}, u32[]{:S(2)}) collective-permute-start(bf16[512,256]{1,0:T(8,128)(2,1)S(1)} %get-tuple-element.35), channel_id=1, source_target_pairs={{0,2},{1,3},{2,0},{3,1},{4,6},{5,7},{6,4},{7,5},{8,10},{9,11},{10,... | collective-permute-start | bytes 786440 | tf_op jit(solution)/shard_map/ocean_sums/ppermute | solution.py:344
  48.7 4.1 %update_of_staying_blocks.4.rest_1_ = bf16[32,1024,128]{2,1,0:T(8,128)(2,1)} custom-call(s32[96]{0:T(128)S(1)} %get-tuple-element.22.order, bf16[7,4,1024,128]{3,2,1,0:T(8,128)(2,1)S(1)} %get-tuple-element.26.kept, bf16[7,1024,512]{2,1,0:T(8,128)(2,1)S(1)} %get-tuple-element.27.hidden, bf16[1024,1024]{1,0:T(8,128)(2,1)S(1)} %get-tuple-element.28.w_out, ...), custom_call_target="tpu_custom_call" | custom-call | flops 2147483648 | bytes 6291456 | tf_op jit(solution)/shard_map/ocean_sums/update_of_staying_blocks/pallas_call | solution.py:436
  52.7 2.8 %collective-permute-done.1.came = bf16[512,256]{1,0:T(8,128)(2,1)S(1)} collective-permute-done((bf16[512,256]{1,0:T(8,128)(2,1)S(1)}, bf16[512,256]{1,0:T(8,128)(2,1)S(1)}, u32[]{:S(2)}, u32[]{:S(2)}) %collective-permute-start.1) | collective-permute-done | bytes 262176 | tf_op jit(solution)/shard_map/ocean_sums/ppermute | solution.py:344
  55.6 2.1 %collective-permute-start.2 = (bf16[256,256]{1,0:T(8,128)(2,1)S(1)}, bf16[256,256]{1,0:T(8,128)(2,1)S(1)}, u32[]{:S(2)}, u32[]{:S(2)}) collective-permute-start(bf16[256,256]{1,0:T(8,128)(2,1)S(1)} %get-tuple-element.37), channel_id=1, source_target_pairs={{0,4},{4,0},{8,12},{12,8},{16,20},{20,16},{24,28},{28,24},{1,5},{5... | collective-permute-start | bytes 393224 | tf_op jit(solution)/shard_map/ocean_sums/ppermute | solution.py:344
  57.6 4.1 %update_of_staying_blocks.5.rest_1_ = bf16[32,1024,128]{2,1,0:T(8,128)(2,1)} custom-call(s32[96]{0:T(128)S(1)} %get-tuple-element.22.order, bf16[7,4,1024,128]{3,2,1,0:T(8,128)(2,1)S(1)} %get-tuple-element.26.kept, bf16[7,1024,512]{2,1,0:T(8,128)(2,1)S(1)} %get-tuple-element.27.hidden, ...), custom_call_target="tpu_custom_call", output_to_operand_aliasing={{}: (5, {})} | custom-call | flops 2147483648 | bytes 6291456 | tf_op jit(solution)/shard_map/ocean_sums/update_of_staying_blocks/pallas_call | solution.py:436
  61.7 0.0 collective-permute-done.2.came
  61.8 4.5 %collective-permute-start.3 = (bf16[128,256]{1,0:T(8,128)(2,1)S(1)}, bf16[128,256]{1,0:T(8,128)(2,1)S(1)}, u32[]{:S(2)}, u32[]{:S(2)}) collective-permute-start(bf16[128,256]{1,0:T(8,128)(2,1)S(1)} %get-tuple-element.39), channel_id=1, source_target_pairs={{0,8},{4,12},{8,0},{12,4},{16,24},{20,28},{24,16},{28,20},{1,9},{5... | collective-permute-start | bytes 196616 | tf_op jit(solution)/shard_map/ocean_sums/ppermute | solution.py:344
  66.3 4.1 %update_of_staying_blocks.6.rest_1_ = bf16[32,1024,128]{2,1,0:T(8,128)(2,1)} custom-call(s32[96]{0:T(128)S(1)} %get-tuple-element.22.order, bf16[7,4,1024,128]{3,2,1,0:T(8,128)(2,1)S(1)} %get-tuple-element.26.kept, bf16[7,1024,512]{2,1,0:T(8,128)(2,1)S(1)} %get-tuple-element.27.hidden, ...), custom_call_target="tpu_custom_call", output_to_operand_aliasing={{}: (5, {})} | custom-call | flops 2147483648 | bytes 6291456 | tf_op jit(solution)/shard_map/ocean_sums/update_of_staying_blocks/pallas_call | solution.py:436
  70.4 2.2 %collective-permute-done.3.came = bf16[128,256]{1,0:T(8,128)(2,1)S(1)} collective-permute-done((bf16[128,256]{1,0:T(8,128)(2,1)S(1)}, bf16[128,256]{1,0:T(8,128)(2,1)S(1)}, u32[]{:S(2)}, u32[]{:S(2)}) %collective-permute-start.3) | collective-permute-done | bytes 65568 | tf_op jit(solution)/shard_map/ocean_sums/ppermute | solution.py:344
  72.6 1.0 %collective-permute-start.4 = (bf16[64,256]{1,0:T(8,128)(2,1)S(1)}, bf16[64,256]{1,0:T(8,128)(2,1)S(1)}, u32[]{:S(2)}, u32[]{:S(2)}) collective-permute-start(bf16[64,256]{1,0:T(8,128)(2,1)S(1)} %get-tuple-element.41), channel_id=1, source_target_pairs={{0,16},{4,20},{8,24},{12,28},{16,0},{20,4},{24,8},{28,12},{1,17},{... | collective-permute-start | bytes 98312 | tf_op jit(solution)/shard_map/ocean_sums/ppermute | solution.py:344
  73.6 2.8 %update_of_staying_blocks.7.partial = bf16[32,1024,128]{2,1,0:T(8,128)(2,1)} custom-call(s32[96]{0:T(128)S(1)} %get-tuple-element.22.order, bf16[7,4,1024,128]{3,2,1,0:T(8,128)(2,1)S(1)} %get-tuple-element.26.kept, bf16[7,1024,512]{2,1,0:T(8,128)(2,1)S(1)} %get-tuple-element.27.hidden, ...), custom_call_target="tpu_custom_call", output_to_operand_aliasing={{}: (5, {})} | custom-call | flops 1073741824 | bytes 4194304 | tf_op jit(solution)/shard_map/ocean_sums/update_of_staying_blocks/pallas_call | solution.py:436
  76.4 1.1 %collective-permute-done.4.came = bf16[64,256]{1,0:T(8,128)(2,1)S(1)} collective-permute-done((bf16[64,256]{1,0:T(8,128)(2,1)S(1)}, bf16[64,256]{1,0:T(8,128)(2,1)S(1)}, u32[]{:S(2)}, u32[]{:S(2)}) %collective-permute-start.4) | collective-permute-done | bytes 32800 | tf_op jit(solution)/shard_map/ocean_sums/ppermute | solution.py:344
  77.5 0.6 ocean_sums.9
  78.1 0.0 all-to-all-done.1.arrived
  78.1 1.5 %arrived_blocks.1 = bf16[32,1024,128]{2,1,0:T(8,128)(2,1)} custom-call(s32[96]{0:T(128)S(1)} %get-tuple-element.22.order, bf16[8,1024,128]{2,1,0:T(8,128)(2,1)S(1)} %all-to-all-done.1.arrived, bf16[32,1024,128]{2,1,0:T(8,128)(2,1)} %update_of_staying_blocks.7.partial), custom_call_target="tpu_custom_call", output_to_operand_aliasing={{}: (2, {})} | custom-call | tf_op jit(solution)/shard_map/arrived_blocks/pallas_call | solution.py:484
  (3 shorter events, 0.1 us)
Async XLA Ops:
  3.1 14.4 %all-to-all-start = ((f32[8,8,128]{2,1,0:T(8,128)}), f32[8,8,128]{2,1,0:T(8,128)S(1)}, u32[]{:S(2)}, u32[]{:S(2)}) async-start(f32[8,8,128]{2,1,0:T(8,128)} %get-tuple-element.24), calls=%async_computation | async-start | bytes 65536 | tf_op jit(solution)/shard_map/all_to_all | solution.py:362
  17.5 60.6 %all-to-all-start.1 = ((bf16[8,1024,128]{2,1,0:T(8,128)(2,1)}), bf16[8,1024,128]{2,1,0:T(8,128)(2,1)S(1)}, u32[]{:S(2)}, u32[]{:S(2)}) async-start(bf16[8,1024,128]{2,1,0:T(8,128)(2,1)} %get-tuple-element.25), calls=%async_computation.1 | async-start | bytes 4194304 | tf_op jit(solution)/shard_map/all_to_all | solution.py:388
  23.5 14.0 %copy-start = (s32[4096,1]{0,1:T(1,128)S(1)}, s32[4096,1]{0,1:T(1,128)}, u32[]{:S(2)}) copy-start(s32[4096,1]{0,1:T(1,128)} %param.13) | copy-start | bytes 49156
  23.5 14.0 %copy-start.1 = (s32[4096]{0:T(1024)S(1)}, s32[4096]{0:T(1024)}, u32[]{:S(2)}) copy-start(s32[4096]{0:T(1024)} %param.14) | copy-start | bytes 49156
  23.5 14.0 %copy-start.2 = (f32[4096]{0:T(1024)S(1)}, f32[4096]{0:T(1024)}, u32[]{:S(2)}) copy-start(f32[4096]{0:T(1024)} %param.15) | copy-start | bytes 49156
  45.0 2.0 %collective-permute-start = (bf16[1024,256]{1,0:T(8,128)(2,1)S(1)}, bf16[1024,256]{1,0:T(8,128)(2,1)S(1)}, u32[]{:S(2)}, u32[]{:S(2)}) collective-permute-start(bf16[1024,256]{1,0:T(8,128)(2,1)S(1)} %get-tuple-element.33), channel_id=1, source_target_pairs={{0,1},{1,0},{2,3},{3,2},{4,5},{5,4},{6,7},{7,6},{8,9},{9,8},{10,11... | collective-permute-start | bytes 1572872 | tf_op jit(solution)/shard_map/ocean_sums/ppermute | solution.py:344
  47.1 8.4 %collective-permute-start.1 = (bf16[512,256]{1,0:T(8,128)(2,1)S(1)}, bf16[512,256]{1,0:T(8,128)(2,1)S(1)}, u32[]{:S(2)}, u32[]{:S(2)}) collective-permute-start(bf16[512,256]{1,0:T(8,128)(2,1)S(1)} %get-tuple-element.35), channel_id=1, source_target_pairs={{0,2},{1,3},{2,0},{3,1},{4,6},{5,7},{6,4},{7,5},{8,10},{9,11},{10,... | collective-permute-start | bytes 786440 | tf_op jit(solution)/shard_map/ocean_sums/ppermute | solution.py:344
  55.6 6.2 %collective-permute-start.2 = (bf16[256,256]{1,0:T(8,128)(2,1)S(1)}, bf16[256,256]{1,0:T(8,128)(2,1)S(1)}, u32[]{:S(2)}, u32[]{:S(2)}) collective-permute-start(bf16[256,256]{1,0:T(8,128)(2,1)S(1)} %get-tuple-element.37), channel_id=1, source_target_pairs={{0,4},{4,0},{8,12},{12,8},{16,20},{20,16},{24,28},{28,24},{1,5},{5... | collective-permute-start | bytes 393224 | tf_op jit(solution)/shard_map/ocean_sums/ppermute | solution.py:344
  61.8 10.8 %collective-permute-start.3 = (bf16[128,256]{1,0:T(8,128)(2,1)S(1)}, bf16[128,256]{1,0:T(8,128)(2,1)S(1)}, u32[]{:S(2)}, u32[]{:S(2)}) collective-permute-start(bf16[128,256]{1,0:T(8,128)(2,1)S(1)} %get-tuple-element.39), channel_id=1, source_target_pairs={{0,8},{4,12},{8,0},{12,4},{16,24},{20,28},{24,16},{28,20},{1,9},{5... | collective-permute-start | bytes 196616 | tf_op jit(solution)/shard_map/ocean_sums/ppermute | solution.py:344
  72.6 4.9 %collective-permute-start.4 = (bf16[64,256]{1,0:T(8,128)(2,1)S(1)}, bf16[64,256]{1,0:T(8,128)(2,1)S(1)}, u32[]{:S(2)}, u32[]{:S(2)}) collective-permute-start(bf16[64,256]{1,0:T(8,128)(2,1)S(1)} %get-tuple-element.41), channel_id=1, source_target_pairs={{0,16},{4,20},{8,24},{12,28},{16,0},{20,4},{24,8},{28,12},{1,17},{... | collective-permute-start | bytes 98312 | tf_op jit(solution)/shard_map/ocean_sums/ppermute | solution.py:344
where the time goes:
time: 80.2 us; the launch traced here: 79.8 us
  Pallas kernels  48.4 us (60%)
  starting transfers between devices  22.5 us (28%)
  waiting for transfers between devices  7.93 us (10%)
  between operations  0.94 us (1%)
    pallas_call x4, Pallas kernels, update(): pl.pallas_call(functools.partial(update_kernel, done, upto), out_shape=sh...  15 us
    pallas_call x1, Pallas kernels, per_device(): pl.pallas_call(hidden_kernel, out_shape=(pltpu.VMEM((groups, inner, side)...  14 us
    ppermute x5, starting transfers between devices, swap(): lax.ppermute(x, axis, [(i, i ^ bit) for i in range(lax.axis_size(axis))])  9.23 us
    ppermute x5, waiting for transfers between devices, swap(): lax.ppermute(x, axis, [(i, i ^ bit) for i in range(lax.axis_size(axis))])  7.93 us
    pallas_call x1, Pallas kernels, per_device(): pl.pallas_call(functools.partial(cells_kernel, devices, nnarrow), out_sha...  7.44 us
    all_to_all x1, starting transfers between devices, per_device(): meta = lax.all_to_all(meta, 'wide', split_axis=0, concat_axis=0, tiled=True)  7.29 us
    pallas_call x1, Pallas kernels, per_device(): pl.pallas_call(leaving_kernel, out_shape=(pltpu.HBM((nwide, depth, cols),...  7.07 us
    all_to_all x1, starting transfers between devices, per_device(): lax.all_to_all(outgoing, 'wide', split_axis=0, concat_axis=0, tiled=True)  6.02 us
  transfers between devices with their start and end apart: 7, of which 4 were waited for; matrix products, arithmetic and copies ran while one was open for 0% of the time, Pallas kernels for 56%

commit v1 on v0

v1 whole, which is shorter than its diff:
```python
import functools

import jax
import jax.numpy as jnp
from jax import lax
from jax.experimental import pallas as pl
from jax.experimental.pallas import tpu as pltpu
from jax.sharding import PartitionSpec as P

OCN_DEV = 512
LANES = 256
GROUP = 4
STEP = 256
CHUNK = 512
MIB = 1024 * 1024


def silu(v):
    u = 0.5 * v
    return u + u * jnp.tanh(u)


def side_by_side(blocks):
    return jnp.concatenate([blocks[j] for j in range(GROUP)], axis=1)


def hidden_of(x, w_in, hid, beside=lambda i: None):
    for i, r in enumerate(range(0, w_in.shape[0], STEP)):
        v = jnp.dot(w_in[r : r + STEP, :], x, preferred_element_type=jnp.float32)
        hid[r : r + STEP, :] = silu(v).astype(jnp.bfloat16)
        beside(i)


def updated(buf_in, hid, w_out, buf_out):
    cols = buf_in.shape[2]
    h = hid[...]
    for r in range(0, w_out.shape[0], STEP):
        t = jnp.dot(w_out[r : r + STEP, :], h, preferred_element_type=jnp.float32)
        for j in range(GROUP):
            old = buf_in[j, r : r + STEP, :].astype(jnp.float32)
            buf_out[j, r : r + STEP, :] = (old + t[:, j * cols : (j + 1) * cols]).astype(jnp.bfloat16)


def arrivals_of(hbm, row_of, vmem, sem, g, b):
    return [
        pltpu.make_async_copy(hbm.at[row_of(g * GROUP + j)], vmem.at[b, j], sem.at[b, j])
        for j in range(GROUP)
    ]


def departures(vmem, hbm, row_of, sem, g, b):
    return [
        pltpu.make_async_copy(vmem.at[b, j], hbm.at[row_of(g * GROUP + j)], sem.at[b, j])
        for j in range(GROUP)
    ]


def start(copies):
    for c in copies:
        c.start()


def wait(copies):
    for c in copies:
        c.wait()


def order_kernel(
    nwide, nnarrow, move, table_hbm, owner_hbm, slot_hbm, weight_hbm, order, meta_hbm,
    table, owner, slot, weight, meta, sem,
):
    blocks = owner.shape[0]
    stay = blocks - move
    pairs = [(table_hbm, table), (owner_hbm, owner), (slot_hbm, slot), (weight_hbm, weight)]
    loads = [pltpu.make_async_copy(src, dst, sem.at[i]) for i, (src, dst) in enumerate(pairs)]
    start(loads)
    me = lax.axis_index("wide")
    base = (me * nnarrow + lax.axis_index("narrow")) * blocks
    loads[0].wait()

    def look(s, counts):
        kept, gone = counts
        dest = lax.div(table[base + s], nnarrow * blocks)
        leaves = dest != me
        order[jnp.where(leaves, stay + gone, kept)] = s
        order[blocks + s] = dest
        order[2 * blocks + s] = lax.rem(2 * me - dest + nwide, nwide)
        step = leaves.astype(jnp.int32)
        return kept + 1 - step, gone + step

    lax.fori_loop(0, blocks, look, (jnp.int32(0), jnp.int32(0)))
    wait(loads[1:])
    meta[...] = jnp.zeros_like(meta)
    for k in range(move):
        s = order[stay + k]
        source = order[2 * blocks + s]
        cell = owner[pl.ds(s, 1), :] * OCN_DEV + slot[pl.ds(s, 1), :]
        meta[source, 0:1, :] = cell.astype(jnp.float32)
        meta[source, 1:2, :] = weight[pl.ds(s, 1), :]
    save = pltpu.make_async_copy(meta, meta_hbm, sem.at[len(pairs)])
    save.start()
    save.wait()


def row_parts(src, dst, sem):
    parts = []
    for i, r in enumerate(range(0, src.shape[0], STEP)):
        rows = pl.ds(r, STEP)
        parts.append(pltpu.make_async_copy(src.at[rows], dst.at[rows], sem.at[i]))
    return parts


def leaving_kernel(
    order, state, w_in_hbm, w_out_hbm, w_flux_hbm, out, flux,
    w_in, w_out, w_flux, buf_in, buf_out, hid, sem_w, sem_f, sem_in, sem_out,
):
    blocks, _, cols = state.shape
    move = flux.shape[0]
    stay = blocks - move

    def slot_of(k):
        return order[stay + k]

    def row_of(k):
        return order[blocks + order[stay + k]]

    groups = move // GROUP
    load_in = row_parts(w_in_hbm, w_in, sem_w.at[0])
    load_out = row_parts(w_out_hbm, w_out, sem_w.at[1])
    load_flux = pltpu.make_async_copy(w_flux_hbm, w_flux, sem_f)
    start(arrivals_of(state, slot_of, buf_in, sem_in, 0, 0))
    start(load_in)
    load_flux.start()
    for g in range(groups):
        b = g % 2
        wait(arrivals_of(state, slot_of, buf_in, sem_in, g, b))
        if g == 0:
            wait(load_in)
            start(load_out)
        if g + 1 < groups:
            start(arrivals_of(state, slot_of, buf_in, sem_in, g + 1, 1 - b))
        if g >= 2:
            wait(departures(buf_out, out, row_of, sem_out, g - 2, b))
        hidden_of(side_by_side(buf_in.at[b]), w_in, hid)
        if g == 0:
            wait(load_out)
        updated(buf_in.at[b], hid, w_out, buf_out.at[b])
        start(departures(buf_out, out, row_of, sem_out, g, b))
        if g == 0:
            load_flux.wait()
        f = jnp.dot(w_flux[...], hid[...], preferred_element_type=jnp.float32)
        for j in range(GROUP):
            flux[g * GROUP + j] = f[:, j * cols : (j + 1) * cols]
    for g in range(max(groups - 2, 0), groups):
        wait(departures(buf_out, out, row_of, sem_out, g, g % 2))


def staying_kernel(
    devices, nnarrow,
    order, state, w_in_hbm, w_out_hbm, w_flux_hbm, flux_away_hbm, meta_hbm, owner_hbm, slot_hbm, weight_hbm,
    hidden, kept, w_out, keep, send,
    w_in, w_flux, flux_away, meta, owner, slot, weight, cells, areas, lows, flux, left, right, total,
    sem_w, sem_s, sem_kept,
):
    groups, _, _, cols = kept.shape
    stay = groups * GROUP
    move = flux_away.shape[0]
    blocks = stay + move
    device = lax.axis_index("wide") * nnarrow + lax.axis_index("narrow")

    def arrivals(g):
        return arrivals_of(state, lambda k: order[k], kept, sem_kept, g, g)

    load_in = row_parts(w_in_hbm, w_in, sem_w.at[0])
    load_out = row_parts(w_out_hbm, w_out, sem_w.at[1])
    pairs = [
        (w_flux_hbm, w_flux), (owner_hbm, owner), (slot_hbm, slot), (weight_hbm, weight),
        (flux_away_hbm, flux_away), (meta_hbm, meta),
    ]
    small = [pltpu.make_async_copy(src, dst, sem_s.at[i]) for i, (src, dst) in enumerate(pairs)]
    start(arrivals(0))
    start(load_in)
    start(small)

    def tables():
        for c in range(blocks):
            here = pl.ds(order[c], 1)
            if c < stay:
                cells[c : c + 1, :] = (owner[here, :] * OCN_DEV + slot[here, :]).astype(jnp.float32)
                areas[c : c + 1, :] = weight[here, :]
            else:
                dest = order[blocks + order[c]]
                cells[c : c + 1, :] = meta[dest, 0:1, :]
                areas[c : c + 1, :] = meta[dest, 1:2, :]
        high, low = spread(devices, device, cells[...].astype(jnp.int32))
        cells[...] = high.astype(jnp.float32)
        lows[...] = low.astype(jnp.float32).T

    def factors(c, at, f):
        if isinstance(c, int):
            row, low = slice(c, c + 1), lows[:, c : c + 1]
        else:
            row = pl.ds(c, 1)
            lane = lax.broadcasted_iota(jnp.int32, (cols, blocks), 1)
            low = jnp.sum(jnp.where(lane == c, lows[...], 0.0), axis=1, keepdims=True)
        fill(at, devices * OCN_DEV // LANES, f, areas[row, :], cells[row, :], low, left, right)

    def one_hot(g, j):
        factors(g * GROUP + j, j * cols, flux[j])

    def work(g, beside):
        hidden_of(side_by_side(kept.at[g]), w_in, hidden.at[g], beside)
        f = jnp.dot(w_flux[...], hidden[g], preferred_element_type=jnp.float32)
        for j in range(GROUP):
            flux[j] = f[:, j * cols : (j + 1) * cols]

    wait(arrivals(0))
    wait(load_in)
    if groups > 1:
        start(arrivals(1))
    wait(small)
    tables()
    work(0, lambda i: None)

    def later(g):
        wait(arrivals(g))
        work(g, lambda i: one_hot(g - 1, i) if i < GROUP else None)

    if devices <= 32:
        for g in range(1, groups):
            if g + 1 < groups:
                start(arrivals(g + 1))
            else:
                start(load_out)
            later(g)
            add_product(total, left, right, g == 1)
    else:
        total[...] = jnp.zeros_like(total)

        @pl.loop(1, groups)
        def _(g):
            @pl.when(g + 1 < groups)
            def _():
                start(arrivals(g + 1))

            @pl.when(g + 1 == groups)
            def _():
                start(load_out)

            later(g)
            add_product(total, left, right, False)

    for j in range(GROUP):
        one_hot(groups - 1, j)
    add_product(total, left, right, False)
    for g in range(move // GROUP):
        for j in range(GROUP):
            k = g * GROUP + j
            factors(stay + k, j * cols, flux_away[k])
        add_product(total, left, right, False)
    half = total.shape[0] // 2
    keep[...] = total[:half, :]
    send[...] = total[half:, :].astype(jnp.bfloat16)
    wait(load_out)


def update_kernel(first, last, order, kept, hidden, w_out, *rest):
    out, buf_out, sem_out = rest[-3:]

    def slot_of(k):
        return order[k]

    @pl.loop(first, last)
    def _(g):
        updated(kept.at[g], hidden.at[g], w_out, buf_out.at[g - first])
        start(departures(buf_out, out, slot_of, sem_out, g, g - first))

    for g in range(first, last):
        wait(departures(buf_out, out, slot_of, sem_out, g, g - first))


def spread(devices, device, cell):
    bits = devices.bit_length() - 1
    apart = (cell // OCN_DEV) ^ device
    far = jnp.zeros_like(apart)
    for i in range(bits):
        far = far | (((apart >> i) & 1) << (bits - 1 - i))
    return far * (OCN_DEV // LANES) + cell % OCN_DEV // LANES, cell % LANES


def fill(at, highs, f, area, high, low, left, right):
    nflux, cols = f.shape
    bf16 = jnp.bfloat16
    f = (f * area).astype(bf16)
    high = jnp.broadcast_to(high, (nflux, cols)).astype(bf16)
    low = jnp.broadcast_to(low, (cols, LANES)).astype(bf16)
    lanes = lax.broadcasted_iota(jnp.int32, (cols, LANES), 1).astype(jnp.float32).astype(bf16)
    one, zero = jnp.ones((), bf16), jnp.zeros((), bf16)
    right[at : at + cols, :] = jnp.where(low == lanes, one, zero)
    for h in range(highs):
        left[h * nflux : (h + 1) * nflux, at : at + cols] = jnp.where(
            high == jnp.asarray(h, bf16), f, zero
        )


def add_product(total, left, right, first):
    h = right[...]
    for r in range(0, total.shape[0], CHUNK):
        p = jnp.dot(left[r : r + CHUNK, :], h, preferred_element_type=jnp.float32)
        total[r : r + CHUNK, :] = p if first else total[r : r + CHUNK, :] + p


def halve_kernel(mine, came, keep, *sends):
    rows = keep.shape[0]
    keep[...] = mine[:rows, :] + came[:rows, :].astype(jnp.float32)
    for i, send in enumerate(sends):
        at = pl.ds((i + 1) * rows, rows)
        send[...] = (mine[at, :] + came[at, :].astype(jnp.float32)).astype(jnp.bfloat16)


def last_kernel(move, order, arrived, mine, *rest):
    came, (_, out, ocean, sem) = rest[:-4], rest[-4:]
    blocks = out.shape[0]
    stay = blocks - move
    copies = []
    for k in range(move):
        s = order[stay + k]
        copies.append(
            pltpu.make_async_copy(arrived.at[order[2 * blocks + s]], out.at[s], sem.at[k])
        )
    start(copies)
    nflux = ocean.shape[0]
    for h in range(OCN_DEV // LANES):
        rows = slice(h * nflux, (h + 1) * nflux)
        part = mine[rows, :]
        for c in came:
            part = part + c[rows, :].astype(jnp.float32)
        ocean[:, h * LANES : (h + 1) * LANES] = part
    wait(copies)


SMEM = pl.BlockSpec(memory_space=pltpu.SMEM)
VMEM = pl.BlockSpec(memory_space=pltpu.VMEM)
HBM = pl.BlockSpec(memory_space=pltpu.HBM)
ANY = pl.BlockSpec(memory_space=pl.ANY)


def per_device(state, group_of, w_in, w_out, w_flux, owner, ocean_slot, remap_weight):
    nwide = lax.axis_size("wide")
    nnarrow = lax.axis_size("narrow")
    blocks, depth, cols = state.shape
    inner = w_in.shape[0]
    nflux = w_flux.shape[0]
    devices = nwide * nnarrow
    move = nwide // 2
    stay = blocks - move
    bf16, f32, i32 = jnp.bfloat16, jnp.float32, jnp.int32
    shape = jax.ShapeDtypeStruct
    dma = pltpu.SemaphoreType.DMA
    side = GROUP * cols
    owner = owner[:, 0].reshape(blocks, cols)
    slot = ocean_slot.reshape(blocks, cols)
    weight = remap_weight.reshape(blocks, cols)
    params = pltpu.CompilerParams(vmem_limit_bytes=20 * MIB)
    in_hbm = functools.partial(pltpu.with_memory_space_constraint, memory_space=pltpu.HBM)
    in_vmem = functools.partial(pltpu.with_memory_space_constraint, memory_space=pltpu.VMEM)

    def cost(n, products):
        return pl.CostEstimate(
            flops=2 * n * cols * inner * depth * products,
            bytes_accessed=4 * n * depth * cols + 2 * inner * depth * products,
            transcendentals=n * cols * inner,
        )

    def swap(x, axis, bit):
        return lax.ppermute(x, axis, [(i, i ^ bit) for i in range(lax.axis_size(axis))])

    with jax.named_scope("order_of_blocks"):
        order, meta = pl.pallas_call(
            functools.partial(order_kernel, nwide, nnarrow, move),
            out_shape=(shape((3 * blocks,), i32), pltpu.HBM((nwide, 8, cols), f32)),
            in_specs=[HBM] * 4,
            out_specs=(SMEM, HBM),
            scratch_shapes=[
                pltpu.SMEM(group_of.shape, i32),
                pltpu.VMEM((blocks, cols), i32),
                pltpu.VMEM((blocks, cols), i32),
                pltpu.VMEM((blocks, cols), f32),
                pltpu.VMEM((nwide, 8, cols), f32),
                dma((5,)),
            ],
            compiler_params=params,
        )(in_hbm(group_of), in_hbm(owner), in_hbm(slot), in_hbm(weight))
    meta = lax.all_to_all(meta, "wide", split_axis=0, concat_axis=0, tiled=True)

    groups = stay // GROUP
    parts = max(inner, depth) // STEP
    with jax.named_scope("leaving_blocks"):
        outgoing, flux_away = pl.pallas_call(
            leaving_kernel,
            out_shape=(pltpu.HBM((nwide, depth, cols), bf16), pltpu.HBM((move, nflux, cols), f32)),
            in_specs=[SMEM, HBM, HBM, HBM, HBM],
            out_specs=(HBM, VMEM),
            scratch_shapes=[
                pltpu.VMEM((inner, depth), bf16),
                pltpu.VMEM((depth, inner), bf16),
                pltpu.VMEM((nflux, inner), bf16),
                pltpu.VMEM((2, GROUP, depth, cols), bf16),
                pltpu.VMEM((2, GROUP, depth, cols), bf16),
                pltpu.VMEM((inner, side), bf16),
                dma((2, parts)),
                dma,
                dma((2, GROUP)),
                dma((2, GROUP)),
            ],
            compiler_params=params,
            cost_estimate=cost(move, 2),
        )(order, in_hbm(state), in_hbm(w_in), in_hbm(w_out), in_hbm(w_flux))
    outgoing, meta = lax.optimization_barrier((outgoing, meta))
    arrived = lax.all_to_all(outgoing, "wide", split_axis=0, concat_axis=0, tiled=True)

    rows = devices * nflux * OCN_DEV // LANES
    with jax.named_scope("staying_blocks_and_cell_sums"):
        hidden, kept, w_out, keep, send = pl.pallas_call(
            functools.partial(staying_kernel, devices, nnarrow),
            out_shape=(
                pltpu.VMEM((groups, inner, side), bf16),
                pltpu.VMEM((groups, GROUP, depth, cols), bf16),
                pltpu.VMEM(w_out.shape, bf16),
                shape((rows // 2, LANES), f32),
                shape((rows // 2, LANES), bf16),
            ),
            in_specs=[SMEM] + [HBM] * 9,
            out_specs=(VMEM,) * 5,
            scratch_shapes=[
                pltpu.VMEM((inner, depth), bf16),
                pltpu.VMEM((nflux, inner), bf16),
                pltpu.VMEM((move, nflux, cols), f32),
                pltpu.VMEM((nwide, 8, cols), f32),
                pltpu.VMEM((blocks, cols), i32),
                pltpu.VMEM((blocks, cols), i32),
                pltpu.VMEM((blocks, cols), f32),
                pltpu.VMEM((blocks, cols), f32),
                pltpu.VMEM((blocks, cols), f32),
                pltpu.VMEM((cols, blocks), f32),
                pltpu.VMEM((GROUP, nflux, cols), f32),
                pltpu.VMEM((rows, side), bf16),
                pltpu.VMEM((side, LANES), bf16),
                pltpu.VMEM((rows, LANES), f32),
                dma((2, parts)),
                dma((6,)),
                dma((groups, GROUP)),
            ],
            compiler_params=pltpu.CompilerParams(vmem_limit_bytes=20 * MIB + 14 * rows * LANES),
            cost_estimate=pl.CostEstimate(
                flops=2 * cols * (stay * inner * depth + rows * LANES * blocks),
                bytes_accessed=2 * stay * depth * cols + 4 * inner * depth,
                transcendentals=stay * cols * inner,
            ),
        )(
            order,
            *map(in_hbm, (state, w_in, w_out, w_flux, flux_away, meta, owner, slot, weight)),
        )

    partial = None
    done = 0

    def update(upto, partial, after):
        begun = () if partial is None else (partial,)
        return pl.pallas_call(
            functools.partial(update_kernel, done, upto),
            out_shape=shape(state.shape, bf16),
            in_specs=[SMEM, VMEM, VMEM, VMEM, ANY] + [ANY] * len(begun),
            out_specs=ANY,
            scratch_shapes=[
                pltpu.VMEM((upto - done, GROUP, depth, cols), bf16),
                dma((upto - done, GROUP)),
            ],
            input_output_aliases={5: 0} if begun else {},
            compiler_params=params,
            cost_estimate=cost((upto - done) * GROUP, 1),
        )(order, in_vmem(kept), in_vmem(hidden), in_vmem(w_out), after, *begun)

    bits = [("narrow", 1 << i) for i in range(nnarrow.bit_length() - 1)]
    bits += [("wide", 1 << i) for i in range(nwide.bit_length() - 3)]
    own = nflux * OCN_DEV // LANES
    rows //= 2
    sends = (send,)
    with jax.named_scope("ocean_sums"):
        for i, (axis, bit) in enumerate(bits):
            came = swap(sends[0], axis, bit)
            if i > 0:
                upto = min(groups, done + -(-groups // len(bits)))
                if upto > done:
                    with jax.named_scope("update_of_staying_blocks"):
                        partial = update(upto, partial, keep)
                    done = upto
            quarters = i == len(bits) - 1
            rows = own if quarters else rows // 2
            count = 3 if quarters else 1
            keep, *sends = pl.pallas_call(
                halve_kernel,
                out_shape=(shape((rows, LANES), f32),) + (shape((rows, LANES), bf16),) * count,
                in_specs=[VMEM, VMEM],
                out_specs=(VMEM,) * (1 + count),
                compiler_params=params,
            )(keep, came)
        came = [swap(x, "wide", d * nwide // 4) for x, d in zip(sends, (2, 1, 3))]
        with jax.named_scope("update_of_staying_blocks"):
            partial = update(groups, partial, keep)

    with jax.named_scope("arrived_blocks_and_last_sums"):
        new_state, ocean = pl.pallas_call(
            functools.partial(last_kernel, move),
            out_shape=(shape(state.shape, bf16), shape((nflux, OCN_DEV), f32)),
            in_specs=[SMEM] + [VMEM] * 5 + [ANY],
            out_specs=(ANY, VMEM),
            scratch_shapes=[dma((move,))],
            input_output_aliases={6: 0},
            compiler_params=params,
        )(order, arrived, keep, *came, partial)
    return (new_state, ocean)


def solution(mesh):
    in_specs = (
        P(("wide", "narrow"), None, None),
        P(),
        P(),
        P(),
        P(),
        P(("wide", "narrow"), None),
        P(("wide", "narrow")),
        P(("wide", "narrow")),
    )
    out_specs = (P(("wide", "narrow"), None, None), P(None, ("wide", "narrow")))
    return jax.shard_map(
        per_device, mesh=mesh, in_specs=in_specs, out_specs=out_specs, check_vma=False
    )
```

time: 80.2 us -> 76.3 us (0.951)
  Pallas kernels: 48.4 us -> 44.2 us
  waiting for transfers between devices: 7.93 us -> 9.39 us
  starting transfers between devices: 22.5 us -> 21.5 us
    pallas_call x8 -> x5, Pallas kernels: 23.8 us -> 21.2 us  [the longest x1 18.9 us: per_device(): pl.pallas_call(functools.partial(staying_kernel, devices, nnarrow), out_s...]
    pallas_call x4 -> x3, Pallas kernels: 15 us -> 13.5 us  [update(): pl.pallas_call(functools.partial(update_kernel, done, upto), out_shape=sh...]
    ppermute x5 -> x6, waiting for transfers between devices: 7.93 us -> 9.39 us  [swap(): lax.ppermute(x, axis, [(i, i ^ bit) for i in range(lax.axis_size(axis))])]
    ppermute x5 -> x6, starting transfers between devices: 9.23 us -> 8.21 us  [swap(): lax.ppermute(x, axis, [(i, i ^ bit) for i in range(lax.axis_size(axis))])]
  transfers between devices with their start and end apart: 7 -> 8, of which waited for: 4 -> 3; matrix products, arithmetic and copies ran while one was open for 0% -> 0% of each run, Pallas kernels for 56% -> 52%
where the time goes in v1:
time: 76.3 us; the launch traced here: 76 us
  Pallas kernels  44.2 us (58%)
  starting transfers between devices  21.5 us (28%)
  waiting for transfers between devices  9.39 us (12%)
  between operations  0.92 us (1%)
    pallas_call x1, Pallas kernels, per_device(): pl.pallas_call(functools.partial(staying_kernel, devices, nnarrow), out_s...  18.9 us
    pallas_call x3, Pallas kernels, update(): pl.pallas_call(functools.partial(update_kernel, done, upto), out_shape=sh...  13.5 us
    ppermute x6, waiting for transfers between devices, swap(): lax.ppermute(x, axis, [(i, i ^ bit) for i in range(lax.axis_size(axis))])  9.39 us
    ppermute x6, starting transfers between devices, swap(): lax.ppermute(x, axis, [(i, i ^ bit) for i in range(lax.axis_size(axis))])  8.21 us
    all_to_all x1, starting transfers between devices, per_device(): meta = lax.all_to_all(meta, 'wide', split_axis=0, concat_axis=0, tiled=True)  7.29 us
    pallas_call x1, Pallas kernels, per_device(): pl.pallas_call(leaving_kernel, out_shape=(pltpu.HBM((nwide, depth, cols),...  6.98 us
    all_to_all x1, starting transfers between devices, per_device(): lax.all_to_all(outgoing, 'wide', split_axis=0, concat_axis=0, tiled=True)  5.97 us
    pallas_call x1, Pallas kernels, per_device(): pl.pallas_call(functools.partial(order_kernel, nwide, nnarrow, move), out...  2.46 us
  transfers between devices with their start and end apart: 8, of which 3 were waited for; matrix products, arithmetic and copies ran while one was open for 0% of the time, Pallas kernels for 52%

profile of v1, /device:TPU:0, one launch (start us, length us, event | category | flops | bytes accessed | tf_op | source)
XLA Modules:
  0.0 76.0 jit_solution(4946510214599772736)
XLA Ops:
  0.6 2.5 %order_of_blocks.1 = (s32[96]{0:T(128)S(1)}, f32[8,8,128]{2,1,0:T(8,128)}) custom-call(s32[1024]{0:T(1024)} %table_hbm.1, s32[32,128]{1,0:T(8,128)} %bitcast.3, s32[32,128]{1,0:T(8,128)} %bitcast.5, f32[32,128]{1,0:T(8,128)} %bitcast.7), custom_call_target="tpu_custom_call" | custom-call | tf_op jit(solution)/shard_map/order_of_blocks/pallas_call | solution.py:379
  3.1 7.3 %all-to-all-start = ((f32[8,8,128]{2,1,0:T(8,128)}), f32[8,8,128]{2,1,0:T(8,128)S(1)}, u32[]{:S(2)}, u32[]{:S(2)}) async-start(f32[8,8,128]{2,1,0:T(8,128)} %get-tuple-element.23), calls=%async_computation | async-start | bytes 65536 | tf_op jit(solution)/shard_map/all_to_all | solution.py:394
  10.4 7.0 %leaving_blocks.1 = (bf16[8,1024,128]{2,1,0:T(8,128)(2,1)}, f32[4,32,128]{2,1,0:T(8,128)}) custom-call(s32[96]{0:T(128)S(1)} %get-tuple-element.21.order, bf16[32,1024,128]{2,1,0:T(8,128)(2,1)} %state.3, bf16[1024,1024]{1,0:T(8,128)(2,1)} %w_in_hbm.3, bf16[1024,1024]{1,0:T(8,128)(2,1)} %w_out_hbm.3, bf16[32,1024]{1,0:T(8,128)(2,1)} %w_flux_hbm.3), custom_call_target="tpu_custom_call" | custom-call | flops 2147483648 | bytes 6291456 | tf_op jit(solution)/shard_map/leaving_blocks/pallas_call | solution.py:399
  17.4 0.0 all-to-all-done.meta_hbm
  17.4 0.0 copy-start
  17.4 6.0 %all-to-all-start.1 = ((bf16[8,1024,128]{2,1,0:T(8,128)(2,1)}), bf16[8,1024,128]{2,1,0:T(8,128)(2,1)S(1)}, u32[]{:S(2)}, u32[]{:S(2)}) async-start(bf16[8,1024,128]{2,1,0:T(8,128)(2,1)} %get-tuple-element.24), calls=%async_computation.1 | async-start | bytes 4194304 | tf_op jit(solution)/shard_map/all_to_all | solution.py:420
  23.4 0.0 copy-done
  23.4 18.9 %staying_blocks_and_cell_sums.1 = (bf16[7,1024,512]{2,1,0:T(8,128)(2,1)S(1)}, bf16[7,4,1024,128]{3,2,1,0:T(8,128)(2,1)S(1)}, bf16[1024,1024]{1,0:T(8,128)(2,1)S(...) custom-call(s32[96]{0:T(128)S(1)} %get-tuple-element.21.order, bf16[32,1024,128]{2,1,0:T(8,128)(2,1)} %state.3, ...), custom_call_target="tpu_custom_call" | custom-call | flops 11811160064 | bytes 11534336 | tf_op jit(solution)/shard_map/staying_blocks_and_cell_sums/pallas_call | solution.py:424
  42.3 0.1 collective-permute-start
  42.3 1.9 %collective-permute-done.came = bf16[1024,256]{1,0:T(8,128)(2,1)S(1)} collective-permute-done((bf16[1024,256]{1,0:T(8,128)(2,1)S(1)}, bf16[1024,256]{1,0:T(8,128)(2,1)S(1)}, u32[]{:S(2)}, u32[]{:S(2)}) %collective-permute-start) | collective-permute-done | bytes 524320 | tf_op jit(solution)/shard_map/ocean_sums/ppermute | solution.py:376
  44.2 0.1 ocean_sums.3
  44.3 1.6 %collective-permute-start.1 = (bf16[512,256]{1,0:T(8,128)(2,1)S(1)}, bf16[512,256]{1,0:T(8,128)(2,1)S(1)}, u32[]{:S(2)}, u32[]{:S(2)}) collective-permute-start(bf16[512,256]{1,0:T(8,128)(2,1)S(1)} %get-tuple-element.30), channel_id=1, source_target_pairs={{0,2},{1,3},{2,0},{3,1},{4,6},{5,7},{6,4},{7,5},{8,10},{9,11},{10,... | collective-permute-start | bytes 786440 | tf_op jit(solution)/shard_map/ocean_sums/ppermute | solution.py:376
  46.0 5.4 %update_of_staying_blocks.3.rest_1_ = bf16[32,1024,128]{2,1,0:T(8,128)(2,1)} custom-call(s32[96]{0:T(128)S(1)} %get-tuple-element.21.order, bf16[7,4,1024,128]{3,2,1,0:T(8,128)(2,1)S(1)} %get-tuple-element.37.kept, bf16[7,1024,512]{2,1,0:T(8,128)(2,1)S(1)} %get-tuple-element.38.hidden, bf16[1024,1024]{1,0:T(8,128)(2,1)S(1)} %get-tuple-element.39.w_out, ...), custom_call_target="tpu_custom_call" | custom-call | flops 3221225472 | bytes 8388608 | tf_op jit(solution)/shard_map/ocean_sums/update_of_staying_blocks/pallas_call | solution.py:470
  51.3 1.4 %collective-permute-done.1.came = bf16[512,256]{1,0:T(8,128)(2,1)S(1)} collective-permute-done((bf16[512,256]{1,0:T(8,128)(2,1)S(1)}, bf16[512,256]{1,0:T(8,128)(2,1)S(1)}, u32[]{:S(2)}, u32[]{:S(2)}) %collective-permute-start.1) | collective-permute-done | bytes 262176 | tf_op jit(solution)/shard_map/ocean_sums/ppermute | solution.py:376
  52.8 2.1 %collective-permute-start.2 = (bf16[256,256]{1,0:T(8,128)(2,1)S(1)}, bf16[256,256]{1,0:T(8,128)(2,1)S(1)}, u32[]{:S(2)}, u32[]{:S(2)}) collective-permute-start(bf16[256,256]{1,0:T(8,128)(2,1)S(1)} %get-tuple-element.32), channel_id=1, source_target_pairs={{0,4},{4,0},{8,12},{12,8},{16,20},{20,16},{24,28},{28,24},{1,5},{5... | collective-permute-start | bytes 393224 | tf_op jit(solution)/shard_map/ocean_sums/ppermute | solution.py:376
  54.9 5.4 %update_of_staying_blocks.4.rest_1_ = bf16[32,1024,128]{2,1,0:T(8,128)(2,1)} custom-call(s32[96]{0:T(128)S(1)} %get-tuple-element.21.order, bf16[7,4,1024,128]{3,2,1,0:T(8,128)(2,1)S(1)} %get-tuple-element.37.kept, bf16[7,1024,512]{2,1,0:T(8,128)(2,1)S(1)} %get-tuple-element.38.hidden, ...), custom_call_target="tpu_custom_call", output_to_operand_aliasing={{}: (5, {})} | custom-call | flops 3221225472 | bytes 8388608 | tf_op jit(solution)/shard_map/ocean_sums/update_of_staying_blocks/pallas_call | solution.py:470
  60.2 0.0 collective-permute-done.2.came
  60.3 2.4 %collective-permute-start.3 = (bf16[64,256]{1,0:T(8,128)(2,1)S(1)}, bf16[64,256]{1,0:T(8,128)(2,1)S(1)}, u32[]{:S(2)}, u32[]{:S(2)}) collective-permute-start(bf16[64,256]{1,0:T(8,128)(2,1)S(1)} %get-tuple-element.34), channel_id=1, source_target_pairs={{0,16},{4,20},{8,24},{12,28},{16,0},{20,4},{24,8},{28,12},{1,17},{... | collective-permute-start | bytes 98312 | tf_op jit(solution)/shard_map/ocean_sums/ppermute | solution.py:376
  62.7 1.5 %collective-permute-start.4 = (bf16[64,256]{1,0:T(8,128)(2,1)S(1)}, bf16[64,256]{1,0:T(8,128)(2,1)S(1)}, u32[]{:S(2)}, u32[]{:S(2)}) collective-permute-start(bf16[64,256]{1,0:T(8,128)(2,1)S(1)} %get-tuple-element.35), channel_id=1, source_target_pairs={{0,8},{4,12},{8,0},{12,4},{16,24},{20,28},{24,16},{28,20},{1,9},{5... | collective-permute-start | bytes 98312 | tf_op jit(solution)/shard_map/ocean_sums/ppermute | solution.py:376
  64.2 0.5 collective-permute-start.5
  64.7 2.8 %update_of_staying_blocks.5.rest_3_ = bf16[32,1024,128]{2,1,0:T(8,128)(2,1)} custom-call(s32[96]{0:T(128)S(1)} %get-tuple-element.21.order, bf16[7,4,1024,128]{3,2,1,0:T(8,128)(2,1)S(1)} %get-tuple-element.37.kept, bf16[7,1024,512]{2,1,0:T(8,128)(2,1)S(1)} %get-tuple-element.38.hidden, ...), custom_call_target="tpu_custom_call", output_to_operand_aliasing={{}: (5, {})} | custom-call | flops 1073741824 | bytes 4194304 | tf_op jit(solution)/shard_map/ocean_sums/update_of_staying_blocks/pallas_call | solution.py:470
  67.5 6.1 %collective-permute-done.3.rest_0_ = bf16[64,256]{1,0:T(8,128)(2,1)S(1)} collective-permute-done((bf16[64,256]{1,0:T(8,128)(2,1)S(1)}, bf16[64,256]{1,0:T(8,128)(2,1)S(1)}, u32[]{:S(2)}, u32[]{:S(2)}) %collective-permute-start.3) | collective-permute-done | bytes 32800 | tf_op jit(solution)/shard_map/ocean_sums/ppermute | solution.py:376
  73.6 0.0 collective-permute-done.4.rest_1_
  73.6 0.0 collective-permute-done.5.rest_2_
  73.6 0.0 all-to-all-done.1.arrived
  73.6 2.2 %arrived_blocks_and_last_sums.1 = (bf16[32,1024,128]{2,1,0:T(8,128)(2,1)}, f32[32,512]{1,0:T(8,128)}) custom-call(s32[96]{0:T(128)S(1)} %get-tuple-element.21.order, bf16[8,1024,128]{2,1,0:T(8,128)(2,1)S(1)} %all-to-all-done.1.arrived, f32[64,256]{1,0:T(8,128)S(1)} %get-tuple-element.33.rest_0_.mine, ...), custom_call_target="tpu_custom_call", output_to_operand_aliasing={{0}: (6, {})} | custom-call | tf_op jit(solution)/shard_map/arrived_blocks_and_last_sums/pallas_call | solution.py:513
  (2 shorter events, 0.1 us)
Async XLA Ops:
  3.1 14.3 %all-to-all-start = ((f32[8,8,128]{2,1,0:T(8,128)}), f32[8,8,128]{2,1,0:T(8,128)S(1)}, u32[]{:S(2)}, u32[]{:S(2)}) async-start(f32[8,8,128]{2,1,0:T(8,128)} %get-tuple-element.23), calls=%async_computation | async-start | bytes 65536 | tf_op jit(solution)/shard_map/all_to_all | solution.py:394
  17.4 6.0 %copy-start = (f32[8,8,128]{2,1,0:T(8,128)}, f32[8,8,128]{2,1,0:T(8,128)S(1)}, u32[]{:S(2)}) copy-start(f32[8,8,128]{2,1,0:T(8,128)S(1)} %all-to-all-done.meta_hbm) | copy-start | bytes 98308
  17.4 56.2 %all-to-all-start.1 = ((bf16[8,1024,128]{2,1,0:T(8,128)(2,1)}), bf16[8,1024,128]{2,1,0:T(8,128)(2,1)S(1)}, u32[]{:S(2)}, u32[]{:S(2)}) async-start(bf16[8,1024,128]{2,1,0:T(8,128)(2,1)} %get-tuple-element.24), calls=%async_computation.1 | async-start | bytes 4194304 | tf_op jit(solution)/shard_map/all_to_all | solution.py:420
  42.3 2.0 %collective-permute-start = (bf16[1024,256]{1,0:T(8,128)(2,1)S(1)}, bf16[1024,256]{1,0:T(8,128)(2,1)S(1)}, u32[]{:S(2)}, u32[]{:S(2)}) collective-permute-start(bf16[1024,256]{1,0:T(8,128)(2,1)S(1)} %get-tuple-element.28), channel_id=1, source_target_pairs={{0,1},{1,0},{2,3},{3,2},{4,5},{5,4},{6,7},{7,6},{8,9},{9,8},{10,11... | collective-permute-start | bytes 1572872 | tf_op jit(solution)/shard_map/ocean_sums/ppermute | solution.py:376
  44.3 8.4 %collective-permute-start.1 = (bf16[512,256]{1,0:T(8,128)(2,1)S(1)}, bf16[512,256]{1,0:T(8,128)(2,1)S(1)}, u32[]{:S(2)}, u32[]{:S(2)}) collective-permute-start(bf16[512,256]{1,0:T(8,128)(2,1)S(1)} %get-tuple-element.30), channel_id=1, source_target_pairs={{0,2},{1,3},{2,0},{3,1},{4,6},{5,7},{6,4},{7,5},{8,10},{9,11},{10,... | collective-permute-start | bytes 786440 | tf_op jit(solution)/shard_map/ocean_sums/ppermute | solution.py:376
  52.8 7.4 %collective-permute-start.2 = (bf16[256,256]{1,0:T(8,128)(2,1)S(1)}, bf16[256,256]{1,0:T(8,128)(2,1)S(1)}, u32[]{:S(2)}, u32[]{:S(2)}) collective-permute-start(bf16[256,256]{1,0:T(8,128)(2,1)S(1)} %get-tuple-element.32), channel_id=1, source_target_pairs={{0,4},{4,0},{8,12},{12,8},{16,20},{20,16},{24,28},{28,24},{1,5},{5... | collective-permute-start | bytes 393224 | tf_op jit(solution)/shard_map/ocean_sums/ppermute | solution.py:376
  60.3 13.3 %collective-permute-start.3 = (bf16[64,256]{1,0:T(8,128)(2,1)S(1)}, bf16[64,256]{1,0:T(8,128)(2,1)S(1)}, u32[]{:S(2)}, u32[]{:S(2)}) collective-permute-start(bf16[64,256]{1,0:T(8,128)(2,1)S(1)} %get-tuple-element.34), channel_id=1, source_target_pairs={{0,16},{4,20},{8,24},{12,28},{16,0},{20,4},{24,8},{28,12},{1,17},{... | collective-permute-start | bytes 98312 | tf_op jit(solution)/shard_map/ocean_sums/ppermute | solution.py:376
  62.7 10.9 %collective-permute-start.4 = (bf16[64,256]{1,0:T(8,128)(2,1)S(1)}, bf16[64,256]{1,0:T(8,128)(2,1)S(1)}, u32[]{:S(2)}, u32[]{:S(2)}) collective-permute-start(bf16[64,256]{1,0:T(8,128)(2,1)S(1)} %get-tuple-element.35), channel_id=1, source_target_pairs={{0,8},{4,12},{8,0},{12,4},{16,24},{20,28},{24,16},{28,20},{1,9},{5... | collective-permute-start | bytes 98312 | tf_op jit(solution)/shard_map/ocean_sums/ppermute | solution.py:376
  64.2 9.4 %collective-permute-start.5 = (bf16[64,256]{1,0:T(8,128)(2,1)S(1)}, bf16[64,256]{1,0:T(8,128)(2,1)S(1)}, u32[]{:S(2)}, u32[]{:S(2)}) collective-permute-start(bf16[64,256]{1,0:T(8,128)(2,1)S(1)} %get-tuple-element.36), channel_id=1, source_target_pairs={{0,24},{4,28},{8,16},{12,20},{16,8},{20,12},{24,0},{28,4},{1,25},{... | collective-permute-start | bytes 98312 | tf_op jit(solution)/shard_map/ocean_sums/ppermute | solution.py:376

commit v2 on v1

--- a/solution.py
+++ b/solution.py
@@ -318,8 +318,7 @@
         send[...] = (mine[at, :] + came[at, :].astype(jnp.float32)).astype(jnp.bfloat16)
 
 
-def last_kernel(move, order, arrived, mine, *rest):
-    came, (_, out, ocean, sem) = rest[:-4], rest[-4:]
+def place_kernel(move, order, arrived, _, out, sem):
     blocks = out.shape[0]
     stay = blocks - move
     copies = []
@@ -329,6 +328,11 @@
             pltpu.make_async_copy(arrived.at[order[2 * blocks + s]], out.at[s], sem.at[k])
         )
     start(copies)
+    wait(copies)
+
+
+def last_kernel(mine, *rest):
+    came, ocean = rest[:-2], rest[-1]
     nflux = ocean.shape[0]
     for h in range(OCN_DEV // LANES):
         rows = slice(h * nflux, (h + 1) * nflux)
@@ -336,7 +340,6 @@
         for c in came:
             part = part + c[rows, :].astype(jnp.float32)
         ocean[:, h * LANES : (h + 1) * LANES] = part
-    wait(copies)
 
 
 SMEM = pl.BlockSpec(memory_space=pltpu.SMEM)
@@ -509,16 +512,24 @@
         with jax.named_scope("update_of_staying_blocks"):
             partial = update(groups, partial, keep)
 
-    with jax.named_scope("arrived_blocks_and_last_sums"):
-        new_state, ocean = pl.pallas_call(
-            functools.partial(last_kernel, move),
-            out_shape=(shape(state.shape, bf16), shape((nflux, OCN_DEV), f32)),
-            in_specs=[SMEM] + [VMEM] * 5 + [ANY],
-            out_specs=(ANY, VMEM),
+    with jax.named_scope("arrived_blocks"):
+        new_state = pl.pallas_call(
+            functools.partial(place_kernel, move),
+            out_shape=shape(state.shape, bf16),
+            in_specs=[SMEM, VMEM, ANY],
+            out_specs=ANY,
             scratch_shapes=[dma((move,))],
-            input_output_aliases={6: 0},
+            input_output_aliases={2: 0},
             compiler_params=params,
-        )(order, arrived, keep, *came, partial)
+        )(order, arrived, partial)
+    with jax.named_scope("last_sums"):
+        ocean = pl.pallas_call(
+            last_kernel,
+            out_shape=shape((nflux, OCN_DEV), f32),
+            in_specs=[VMEM] * 4 + [ANY],
+            out_specs=VMEM,
+            compiler_params=params,
+        )(keep, *came, new_state)
     return (new_state, ocean)
 
 

time: 76.3 us -> 79.2 us (1.038)
  local copies, waits for them, and re-layouts: 0.01 us -> 3.38 us
    ppermute x6, waiting for transfers between devices: 9.39 us -> 3.42 us  [swap(): lax.ppermute(x, axis, [(i, i ^ bit) for i in range(lax.axis_size(axis))])]
    all_to_all x1, waiting for transfers between devices: 0.01 us -> 5.67 us  [per_device(): lax.all_to_all(outgoing, 'wide', split_axis=0, concat_axis=0, tiled=True)]
    unnamed x2 -> x4, local copies, waits for them, and re-layouts: 0.01 us -> 3.38 us
    pallas_call x1 -> x2, Pallas kernels: 2.18 us -> 2.19 us  [the longest x1 1.54 us: per_device(): pl.pallas_call(functools.partial(place_kernel, move), out_shape=shape(sta...]
where the time goes in v2:
time: 79.2 us; the launch traced here: 78.8 us
  Pallas kernels  44.1 us (56%)
  starting transfers between devices  21.4 us (27%)
  waiting for transfers between devices  9.1 us (11%)
  local copies, waits for them, and re-layouts  3.38 us (4%)
    pallas_call x1, Pallas kernels, per_device(): pl.pallas_call(functools.partial(staying_kernel, devices, nnarrow), out_s...  18.8 us
    pallas_call x3, Pallas kernels, update(): pl.pallas_call(functools.partial(update_kernel, done, upto), out_shape=sh...  13.5 us
    ppermute x6, starting transfers between devices, swap(): lax.ppermute(x, axis, [(i, i ^ bit) for i in range(lax.axis_size(axis))])  8.12 us
    all_to_all x1, starting transfers between devices, per_device(): meta = lax.all_to_all(meta, 'wide', split_axis=0, concat_axis=0, tiled=True)  7.29 us
    pallas_call x1, Pallas kernels, per_device(): pl.pallas_call(leaving_kernel, out_shape=(pltpu.HBM((nwide, depth, cols),...  6.99 us
    all_to_all x1, starting transfers between devices, per_device(): lax.all_to_all(outgoing, 'wide', split_axis=0, concat_axis=0, tiled=True)  6.03 us
    all_to_all x1, waiting for transfers between devices, per_device(): lax.all_to_all(outgoing, 'wide', split_axis=0, concat_axis=0, tiled=True)  5.67 us
    ppermute x6, waiting for transfers between devices, swap(): lax.ppermute(x, axis, [(i, i ^ bit) for i in range(lax.axis_size(axis))])  3.42 us
  transfers between devices with their start and end apart: 8, of which 3 were waited for; matrix products, arithmetic and copies ran while one was open for 0% of the time, Pallas kernels for 52%

profile of v2, /device:TPU:0, one launch (start us, length us, event | category | flops | bytes accessed | tf_op | source)
XLA Modules:
  0.0 78.8 jit_solution(974941951383898779)
XLA Ops:
  0.6 2.5 %order_of_blocks.1 = (s32[96]{0:T(128)S(1)}, f32[8,8,128]{2,1,0:T(8,128)}) custom-call(s32[1024]{0:T(1024)} %table_hbm.1, s32[32,128]{1,0:T(8,128)} %bitcast.3, s32[32,128]{1,0:T(8,128)} %bitcast.5, f32[32,128]{1,0:T(8,128)} %bitcast.7), custom_call_target="tpu_custom_call" | custom-call | tf_op jit(solution)/shard_map/order_of_blocks/pallas_call | solution.py:382
  3.1 7.3 %all-to-all-start = ((f32[8,8,128]{2,1,0:T(8,128)}), f32[8,8,128]{2,1,0:T(8,128)S(1)}, u32[]{:S(2)}, u32[]{:S(2)}) async-start(f32[8,8,128]{2,1,0:T(8,128)} %get-tuple-element.23), calls=%async_computation | async-start | bytes 65536 | tf_op jit(solution)/shard_map/all_to_all | solution.py:397
  10.4 7.0 %leaving_blocks.1 = (bf16[8,1024,128]{2,1,0:T(8,128)(2,1)}, f32[4,32,128]{2,1,0:T(8,128)}) custom-call(s32[96]{0:T(128)S(1)} %get-tuple-element.21.order, bf16[32,1024,128]{2,1,0:T(8,128)(2,1)} %state.3, bf16[1024,1024]{1,0:T(8,128)(2,1)} %w_in_hbm.3, bf16[1024,1024]{1,0:T(8,128)(2,1)} %w_out_hbm.3, bf16[32,1024]{1,0:T(8,128)(2,1)} %w_flux_hbm.3), custom_call_target="tpu_custom_call" | custom-call | flops 2147483648 | bytes 6291456 | tf_op jit(solution)/shard_map/leaving_blocks/pallas_call | solution.py:402
  17.4 0.0 all-to-all-done.meta_hbm
  17.4 0.0 copy-start.1
  17.4 6.0 %all-to-all-start.1 = ((bf16[8,1024,128]{2,1,0:T(8,128)(2,1)}), bf16[8,1024,128]{2,1,0:T(8,128)(2,1)S(1)}, u32[]{:S(2)}, u32[]{:S(2)}) async-start(bf16[8,1024,128]{2,1,0:T(8,128)(2,1)} %get-tuple-element.24), calls=%async_computation.1 | async-start | bytes 4194304 | tf_op jit(solution)/shard_map/all_to_all | solution.py:423
  23.4 0.0 copy-done.1
  23.4 18.8 %staying_blocks_and_cell_sums.1 = (bf16[7,1024,512]{2,1,0:T(8,128)(2,1)S(1)}, bf16[7,4,1024,128]{3,2,1,0:T(8,128)(2,1)S(1)}, bf16[1024,1024]{1,0:T(8,128)(2,1)S(...) custom-call(s32[96]{0:T(128)S(1)} %get-tuple-element.21.order, bf16[32,1024,128]{2,1,0:T(8,128)(2,1)} %state.3, ...), custom_call_target="tpu_custom_call" | custom-call | flops 11811160064 | bytes 11534336 | tf_op jit(solution)/shard_map/staying_blocks_and_cell_sums/pallas_call | solution.py:427
  42.3 0.1 collective-permute-start
  42.3 1.9 %collective-permute-done.came = bf16[1024,256]{1,0:T(8,128)(2,1)S(1)} collective-permute-done((bf16[1024,256]{1,0:T(8,128)(2,1)S(1)}, bf16[1024,256]{1,0:T(8,128)(2,1)S(1)}, u32[]{:S(2)}, u32[]{:S(2)}) %collective-permute-start) | collective-permute-done | bytes 524320 | tf_op jit(solution)/shard_map/ocean_sums/ppermute | solution.py:379
  44.2 0.1 ocean_sums.3
  44.3 1.5 %collective-permute-start.1 = (bf16[512,256]{1,0:T(8,128)(2,1)S(1)}, bf16[512,256]{1,0:T(8,128)(2,1)S(1)}, u32[]{:S(2)}, u32[]{:S(2)}) collective-permute-start(bf16[512,256]{1,0:T(8,128)(2,1)S(1)} %get-tuple-element.33), channel_id=1, source_target_pairs={{0,2},{1,3},{2,0},{3,1},{4,6},{5,7},{6,4},{7,5},{8,10},{9,11},{10,... | collective-permute-start | bytes 786440 | tf_op jit(solution)/shard_map/ocean_sums/ppermute | solution.py:379
  45.9 5.4 %update_of_staying_blocks.3.rest_1_ = bf16[32,1024,128]{2,1,0:T(8,128)(2,1)} custom-call(s32[96]{0:T(128)S(1)} %get-tuple-element.21.order, bf16[7,4,1024,128]{3,2,1,0:T(8,128)(2,1)S(1)} %get-tuple-element.27.kept, bf16[7,1024,512]{2,1,0:T(8,128)(2,1)S(1)} %get-tuple-element.28.hidden, bf16[1024,1024]{1,0:T(8,128)(2,1)S(1)} %get-tuple-element.29.w_out, ...), custom_call_target="tpu_custom_call" | custom-call | flops 3221225472 | bytes 8388608 | tf_op jit(solution)/shard_map/ocean_sums/update_of_staying_blocks/pallas_call | solution.py:473
  51.2 1.5 %collective-permute-done.1.came = bf16[512,256]{1,0:T(8,128)(2,1)S(1)} collective-permute-done((bf16[512,256]{1,0:T(8,128)(2,1)S(1)}, bf16[512,256]{1,0:T(8,128)(2,1)S(1)}, u32[]{:S(2)}, u32[]{:S(2)}) %collective-permute-start.1) | collective-permute-done | bytes 262176 | tf_op jit(solution)/shard_map/ocean_sums/ppermute | solution.py:379
  52.8 2.1 %collective-permute-start.2 = (bf16[256,256]{1,0:T(8,128)(2,1)S(1)}, bf16[256,256]{1,0:T(8,128)(2,1)S(1)}, u32[]{:S(2)}, u32[]{:S(2)}) collective-permute-start(bf16[256,256]{1,0:T(8,128)(2,1)S(1)} %get-tuple-element.35), channel_id=1, source_target_pairs={{0,4},{4,0},{8,12},{12,8},{16,20},{20,16},{24,28},{28,24},{1,5},{5... | collective-permute-start | bytes 393224 | tf_op jit(solution)/shard_map/ocean_sums/ppermute | solution.py:379
  54.9 5.4 %update_of_staying_blocks.4.rest_1_ = bf16[32,1024,128]{2,1,0:T(8,128)(2,1)} custom-call(s32[96]{0:T(128)S(1)} %get-tuple-element.21.order, bf16[7,4,1024,128]{3,2,1,0:T(8,128)(2,1)S(1)} %get-tuple-element.27.kept, bf16[7,1024,512]{2,1,0:T(8,128)(2,1)S(1)} %get-tuple-element.28.hidden, ...), custom_call_target="tpu_custom_call", output_to_operand_aliasing={{}: (5, {})} | custom-call | flops 3221225472 | bytes 8388608 | tf_op jit(solution)/shard_map/ocean_sums/update_of_staying_blocks/pallas_call | solution.py:473
  60.3 0.0 collective-permute-done.2.came
  60.3 2.4 %collective-permute-start.3 = (bf16[64,256]{1,0:T(8,128)(2,1)S(1)}, bf16[64,256]{1,0:T(8,128)(2,1)S(1)}, u32[]{:S(2)}, u32[]{:S(2)}) collective-permute-start(bf16[64,256]{1,0:T(8,128)(2,1)S(1)} %get-tuple-element.37), channel_id=1, source_target_pairs={{0,16},{4,20},{8,24},{12,28},{16,0},{20,4},{24,8},{28,12},{1,17},{... | collective-permute-start | bytes 98312 | tf_op jit(solution)/shard_map/ocean_sums/ppermute | solution.py:379
  62.7 1.5 %collective-permute-start.4 = (bf16[64,256]{1,0:T(8,128)(2,1)S(1)}, bf16[64,256]{1,0:T(8,128)(2,1)S(1)}, u32[]{:S(2)}, u32[]{:S(2)}) collective-permute-start(bf16[64,256]{1,0:T(8,128)(2,1)S(1)} %get-tuple-element.38), channel_id=1, source_target_pairs={{0,8},{4,12},{8,0},{12,4},{16,24},{20,28},{24,16},{28,20},{1,9},{5... | collective-permute-start | bytes 98312 | tf_op jit(solution)/shard_map/ocean_sums/ppermute | solution.py:379
  64.2 0.6 collective-permute-start.5
  64.8 2.8 %update_of_staying_blocks.5._ = bf16[32,1024,128]{2,1,0:T(8,128)(2,1)} custom-call(s32[96]{0:T(128)S(1)} %get-tuple-element.21.order, bf16[7,4,1024,128]{3,2,1,0:T(8,128)(2,1)S(1)} %get-tuple-element.27.kept, bf16[7,1024,512]{2,1,0:T(8,128)(2,1)S(1)} %get-tuple-element.28.hidden, ...), custom_call_target="tpu_custom_call", output_to_operand_aliasing={{}: (5, {})} | custom-call | flops 1073741824 | bytes 4194304 | tf_op jit(solution)/shard_map/ocean_sums/update_of_staying_blocks/pallas_call | solution.py:473
  67.5 5.7 %all-to-all-done.1.arrived = bf16[8,1024,128]{2,1,0:T(8,128)(2,1)S(1)} async-done(((bf16[8,1024,128]{2,1,0:T(8,128)(2,1)}), bf16[8,1024,128]{2,1,0:T(8,128)(2,1)S(1)}, u32[]{:S(2)}, u32[]{:S(2)}) %all-to-all-start.1) | async-done | bytes 2097184 | tf_op jit(solution)/shard_map/all_to_all | solution.py:423
  73.2 1.5 %arrived_blocks.1.rest_3_ = bf16[32,1024,128]{2,1,0:T(8,128)(2,1)} custom-call(s32[96]{0:T(128)S(1)} %get-tuple-element.21.order, bf16[8,1024,128]{2,1,0:T(8,128)(2,1)S(1)} %all-to-all-done.1.arrived, bf16[32,1024,128]{2,1,0:T(8,128)(2,1)} %update_of_staying_blocks.5._), custom_call_target="tpu_custom_call", output_to_operand_aliasing={{}: (2, {})} | custom-call | tf_op jit(solution)/shard_map/arrived_blocks/pallas_call | solution.py:516
  74.8 0.0 collective-permute-done.3.rest_0_
  74.8 0.0 collective-permute-done.4.rest_1_
  74.8 0.0 collective-permute-done.5.rest_2_
  74.8 0.0 copy-start
  74.8 3.4 %copy-done = bf16[32,1024,128]{2,1,0:T(8,128)(2,1)S(1)} copy-done((bf16[32,1024,128]{2,1,0:T(8,128)(2,1)S(1)}, bf16[32,1024,128]{2,1,0:T(8,128)(2,1)}, u32[]{:S(2)}) %copy-start) | copy-done | bytes 8388632
  78.2 0.6 last_sums.1
  (2 shorter events, 0.1 us)
Async XLA Ops:
  3.1 14.3 %all-to-all-start = ((f32[8,8,128]{2,1,0:T(8,128)}), f32[8,8,128]{2,1,0:T(8,128)S(1)}, u32[]{:S(2)}, u32[]{:S(2)}) async-start(f32[8,8,128]{2,1,0:T(8,128)} %get-tuple-element.23), calls=%async_computation | async-start | bytes 65536 | tf_op jit(solution)/shard_map/all_to_all | solution.py:397
  17.4 6.0 %copy-start.1 = (f32[8,8,128]{2,1,0:T(8,128)}, f32[8,8,128]{2,1,0:T(8,128)S(1)}, u32[]{:S(2)}) copy-start(f32[8,8,128]{2,1,0:T(8,128)S(1)} %all-to-all-done.meta_hbm) | copy-start | bytes 98308
  17.4 55.8 %all-to-all-start.1 = ((bf16[8,1024,128]{2,1,0:T(8,128)(2,1)}), bf16[8,1024,128]{2,1,0:T(8,128)(2,1)S(1)}, u32[]{:S(2)}, u32[]{:S(2)}) async-start(bf16[8,1024,128]{2,1,0:T(8,128)(2,1)} %get-tuple-element.24), calls=%async_computation.1 | async-start | bytes 4194304 | tf_op jit(solution)/shard_map/all_to_all | solution.py:423
  42.3 2.0 %collective-permute-start = (bf16[1024,256]{1,0:T(8,128)(2,1)S(1)}, bf16[1024,256]{1,0:T(8,128)(2,1)S(1)}, u32[]{:S(2)}, u32[]{:S(2)}) collective-permute-start(bf16[1024,256]{1,0:T(8,128)(2,1)S(1)} %get-tuple-element.31), channel_id=1, source_target_pairs={{0,1},{1,0},{2,3},{3,2},{4,5},{5,4},{6,7},{7,6},{8,9},{9,8},{10,11... | collective-permute-start | bytes 1572872 | tf_op jit(solution)/shard_map/ocean_sums/ppermute | solution.py:379
  44.3 8.4 %collective-permute-start.1 = (bf16[512,256]{1,0:T(8,128)(2,1)S(1)}, bf16[512,256]{1,0:T(8,128)(2,1)S(1)}, u32[]{:S(2)}, u32[]{:S(2)}) collective-permute-start(bf16[512,256]{1,0:T(8,128)(2,1)S(1)} %get-tuple-element.33), channel_id=1, source_target_pairs={{0,2},{1,3},{2,0},{3,1},{4,6},{5,7},{6,4},{7,5},{8,10},{9,11},{10,... | collective-permute-start | bytes 786440 | tf_op jit(solution)/shard_map/ocean_sums/ppermute | solution.py:379
  52.8 7.5 %collective-permute-start.2 = (bf16[256,256]{1,0:T(8,128)(2,1)S(1)}, bf16[256,256]{1,0:T(8,128)(2,1)S(1)}, u32[]{:S(2)}, u32[]{:S(2)}) collective-permute-start(bf16[256,256]{1,0:T(8,128)(2,1)S(1)} %get-tuple-element.35), channel_id=1, source_target_pairs={{0,4},{4,0},{8,12},{12,8},{16,20},{20,16},{24,28},{28,24},{1,5},{5... | collective-permute-start | bytes 393224 | tf_op jit(solution)/shard_map/ocean_sums/ppermute | solution.py:379
  60.3 14.5 %collective-permute-start.3 = (bf16[64,256]{1,0:T(8,128)(2,1)S(1)}, bf16[64,256]{1,0:T(8,128)(2,1)S(1)}, u32[]{:S(2)}, u32[]{:S(2)}) collective-permute-start(bf16[64,256]{1,0:T(8,128)(2,1)S(1)} %get-tuple-element.37), channel_id=1, source_target_pairs={{0,16},{4,20},{8,24},{12,28},{16,0},{20,4},{24,8},{28,12},{1,17},{... | collective-permute-start | bytes 98312 | tf_op jit(solution)/shard_map/ocean_sums/ppermute | solution.py:379
  62.7 12.1 %collective-permute-start.4 = (bf16[64,256]{1,0:T(8,128)(2,1)S(1)}, bf16[64,256]{1,0:T(8,128)(2,1)S(1)}, u32[]{:S(2)}, u32[]{:S(2)}) collective-permute-start(bf16[64,256]{1,0:T(8,128)(2,1)S(1)} %get-tuple-element.38), channel_id=1, source_target_pairs={{0,8},{4,12},{8,0},{12,4},{16,24},{20,28},{24,16},{28,20},{1,9},{5... | collective-permute-start | bytes 98312 | tf_op jit(solution)/shard_map/ocean_sums/ppermute | solution.py:379
  64.2 10.6 %collective-permute-start.5 = (bf16[64,256]{1,0:T(8,128)(2,1)S(1)}, bf16[64,256]{1,0:T(8,128)(2,1)S(1)}, u32[]{:S(2)}, u32[]{:S(2)}) collective-permute-start(bf16[64,256]{1,0:T(8,128)(2,1)S(1)} %get-tuple-element.39), channel_id=1, source_target_pairs={{0,24},{4,28},{8,16},{12,20},{16,8},{20,12},{24,0},{28,4},{1,25},{... | collective-permute-start | bytes 98312 | tf_op jit(solution)/shard_map/ocean_sums/ppermute | solution.py:379
  74.8 3.4 %copy-start = (bf16[32,1024,128]{2,1,0:T(8,128)(2,1)S(1)}, bf16[32,1024,128]{2,1,0:T(8,128)(2,1)}, u32[]{:S(2)}) copy-start(bf16[32,1024,128]{2,1,0:T(8,128)(2,1)} %arrived_blocks.1.rest_3_) | copy-start | bytes 25165828

commit v3 on v2

--- a/solution.py
+++ b/solution.py
@@ -526,10 +526,10 @@
         ocean = pl.pallas_call(
             last_kernel,
             out_shape=shape((nflux, OCN_DEV), f32),
-            in_specs=[VMEM] * 4 + [ANY],
+            in_specs=[VMEM] * 4 + [HBM],
             out_specs=VMEM,
             compiler_params=params,
-        )(keep, *came, new_state)
+        )(keep, *came, in_hbm(new_state))
     return (new_state, ocean)
 
 

time: 79.2 us -> 75.8 us (0.957)
  local copies, waits for them, and re-layouts: 3.38 us -> 0.01 us
    unnamed x4 -> x2, local copies, waits for them, and re-layouts: 3.38 us -> 0.01 us
  transfers between devices with their start and end apart: 8 -> 8, of which waited for: 3 -> 3; matrix products, arithmetic and copies ran while one was open for 0% -> 0% of each run, Pallas kernels for 52% -> 54%
where the time goes in v3:
time: 75.8 us; the launch traced here: 75.5 us
  Pallas kernels  44.2 us (58%)
  starting transfers between devices  21.4 us (28%)
  waiting for transfers between devices  9.14 us (12%)
  between operations  0.76 us (1%)
    pallas_call x1, Pallas kernels, per_device(): pl.pallas_call(functools.partial(staying_kernel, devices, nnarrow), out_s...  18.8 us
    pallas_call x3, Pallas kernels, update(): pl.pallas_call(functools.partial(update_kernel, done, upto), out_shape=sh...  13.5 us
    ppermute x6, starting transfers between devices, swap(): lax.ppermute(x, axis, [(i, i ^ bit) for i in range(lax.axis_size(axis))])  8.14 us
    all_to_all x1, starting transfers between devices, per_device(): meta = lax.all_to_all(meta, 'wide', split_axis=0, concat_axis=0, tiled=True)  7.29 us
    pallas_call x1, Pallas kernels, per_device(): pl.pallas_call(leaving_kernel, out_shape=(pltpu.HBM((nwide, depth, cols),...  6.99 us
    all_to_all x1, starting transfers between devices, per_device(): lax.all_to_all(outgoing, 'wide', split_axis=0, concat_axis=0, tiled=True)  5.97 us
    all_to_all x1, waiting for transfers between devices, per_device(): lax.all_to_all(outgoing, 'wide', split_axis=0, concat_axis=0, tiled=True)  5.74 us
    ppermute x6, waiting for transfers between devices, swap(): lax.ppermute(x, axis, [(i, i ^ bit) for i in range(lax.axis_size(axis))])  3.4 us
  transfers between devices with their start and end apart: 8, of which 3 were waited for; matrix products, arithmetic and copies ran while one was open for 0% of the time, Pallas kernels for 54%

profile of v3, /device:TPU:0, one launch (start us, length us, event | category | flops | bytes accessed | tf_op | source)
XLA Modules:
  0.0 75.5 jit_solution(9757988480347798414)
XLA Ops:
  0.6 2.5 %order_of_blocks.1 = (s32[96]{0:T(128)S(1)}, f32[8,8,128]{2,1,0:T(8,128)}) custom-call(s32[1024]{0:T(1024)} %table_hbm.1, s32[32,128]{1,0:T(8,128)} %bitcast.3, s32[32,128]{1,0:T(8,128)} %bitcast.5, f32[32,128]{1,0:T(8,128)} %bitcast.7), custom_call_target="tpu_custom_call" | custom-call | tf_op jit(solution)/shard_map/order_of_blocks/pallas_call | solution.py:382
  3.1 7.3 %all-to-all-start = ((f32[8,8,128]{2,1,0:T(8,128)}), f32[8,8,128]{2,1,0:T(8,128)S(1)}, u32[]{:S(2)}, u32[]{:S(2)}) async-start(f32[8,8,128]{2,1,0:T(8,128)} %get-tuple-element.23), calls=%async_computation | async-start | bytes 65536 | tf_op jit(solution)/shard_map/all_to_all | solution.py:397
  10.4 7.0 %leaving_blocks.1 = (bf16[8,1024,128]{2,1,0:T(8,128)(2,1)}, f32[4,32,128]{2,1,0:T(8,128)}) custom-call(s32[96]{0:T(128)S(1)} %get-tuple-element.21.order, bf16[32,1024,128]{2,1,0:T(8,128)(2,1)} %state.3, bf16[1024,1024]{1,0:T(8,128)(2,1)} %w_in_hbm.3, bf16[1024,1024]{1,0:T(8,128)(2,1)} %w_out_hbm.3, bf16[32,1024]{1,0:T(8,128)(2,1)} %w_flux_hbm.3), custom_call_target="tpu_custom_call" | custom-call | flops 2147483648 | bytes 6291456 | tf_op jit(solution)/shard_map/leaving_blocks/pallas_call | solution.py:402
  17.4 0.0 all-to-all-done.meta_hbm
  17.4 0.0 copy-start
  17.4 6.0 %all-to-all-start.1 = ((bf16[8,1024,128]{2,1,0:T(8,128)(2,1)}), bf16[8,1024,128]{2,1,0:T(8,128)(2,1)S(1)}, u32[]{:S(2)}, u32[]{:S(2)}) async-start(bf16[8,1024,128]{2,1,0:T(8,128)(2,1)} %get-tuple-element.24), calls=%async_computation.1 | async-start | bytes 4194304 | tf_op jit(solution)/shard_map/all_to_all | solution.py:423
  23.4 0.0 copy-done
  23.4 18.8 %staying_blocks_and_cell_sums.1 = (bf16[7,1024,512]{2,1,0:T(8,128)(2,1)S(1)}, bf16[7,4,1024,128]{3,2,1,0:T(8,128)(2,1)S(1)}, bf16[1024,1024]{1,0:T(8,128)(2,1)S(...) custom-call(s32[96]{0:T(128)S(1)} %get-tuple-element.21.order, bf16[32,1024,128]{2,1,0:T(8,128)(2,1)} %state.3, ...), custom_call_target="tpu_custom_call" | custom-call | flops 11811160064 | bytes 11534336 | tf_op jit(solution)/shard_map/staying_blocks_and_cell_sums/pallas_call | solution.py:427
  42.2 0.1 collective-permute-start
  42.3 1.9 %collective-permute-done.came = bf16[1024,256]{1,0:T(8,128)(2,1)S(1)} collective-permute-done((bf16[1024,256]{1,0:T(8,128)(2,1)S(1)}, bf16[1024,256]{1,0:T(8,128)(2,1)S(1)}, u32[]{:S(2)}, u32[]{:S(2)}) %collective-permute-start) | collective-permute-done | bytes 524320 | tf_op jit(solution)/shard_map/ocean_sums/ppermute | solution.py:379
  44.2 0.1 ocean_sums.3
  44.3 1.5 %collective-permute-start.1 = (bf16[512,256]{1,0:T(8,128)(2,1)S(1)}, bf16[512,256]{1,0:T(8,128)(2,1)S(1)}, u32[]{:S(2)}, u32[]{:S(2)}) collective-permute-start(bf16[512,256]{1,0:T(8,128)(2,1)S(1)} %get-tuple-element.33), channel_id=1, source_target_pairs={{0,2},{1,3},{2,0},{3,1},{4,6},{5,7},{6,4},{7,5},{8,10},{9,11},{10,... | collective-permute-start | bytes 786440 | tf_op jit(solution)/shard_map/ocean_sums/ppermute | solution.py:379
  45.8 5.4 %update_of_staying_blocks.3.rest_1_ = bf16[32,1024,128]{2,1,0:T(8,128)(2,1)} custom-call(s32[96]{0:T(128)S(1)} %get-tuple-element.21.order, bf16[7,4,1024,128]{3,2,1,0:T(8,128)(2,1)S(1)} %get-tuple-element.27.kept, bf16[7,1024,512]{2,1,0:T(8,128)(2,1)S(1)} %get-tuple-element.28.hidden, bf16[1024,1024]{1,0:T(8,128)(2,1)S(1)} %get-tuple-element.29.w_out, ...), custom_call_target="tpu_custom_call" | custom-call | flops 3221225472 | bytes 8388608 | tf_op jit(solution)/shard_map/ocean_sums/update_of_staying_blocks/pallas_call | solution.py:473
  51.2 1.5 %collective-permute-done.1.came = bf16[512,256]{1,0:T(8,128)(2,1)S(1)} collective-permute-done((bf16[512,256]{1,0:T(8,128)(2,1)S(1)}, bf16[512,256]{1,0:T(8,128)(2,1)S(1)}, u32[]{:S(2)}, u32[]{:S(2)}) %collective-permute-start.1) | collective-permute-done | bytes 262176 | tf_op jit(solution)/shard_map/ocean_sums/ppermute | solution.py:379
  52.8 2.1 %collective-permute-start.2 = (bf16[256,256]{1,0:T(8,128)(2,1)S(1)}, bf16[256,256]{1,0:T(8,128)(2,1)S(1)}, u32[]{:S(2)}, u32[]{:S(2)}) collective-permute-start(bf16[256,256]{1,0:T(8,128)(2,1)S(1)} %get-tuple-element.35), channel_id=1, source_target_pairs={{0,4},{4,0},{8,12},{12,8},{16,20},{20,16},{24,28},{28,24},{1,5},{5... | collective-permute-start | bytes 393224 | tf_op jit(solution)/shard_map/ocean_sums/ppermute | solution.py:379
  54.8 5.4 %update_of_staying_blocks.4.rest_1_ = bf16[32,1024,128]{2,1,0:T(8,128)(2,1)} custom-call(s32[96]{0:T(128)S(1)} %get-tuple-element.21.order, bf16[7,4,1024,128]{3,2,1,0:T(8,128)(2,1)S(1)} %get-tuple-element.27.kept, bf16[7,1024,512]{2,1,0:T(8,128)(2,1)S(1)} %get-tuple-element.28.hidden, ...), custom_call_target="tpu_custom_call", output_to_operand_aliasing={{}: (5, {})} | custom-call | flops 3221225472 | bytes 8388608 | tf_op jit(solution)/shard_map/ocean_sums/update_of_staying_blocks/pallas_call | solution.py:473
  60.2 0.0 collective-permute-done.2.came
  60.3 2.4 %collective-permute-start.3 = (bf16[64,256]{1,0:T(8,128)(2,1)S(1)}, bf16[64,256]{1,0:T(8,128)(2,1)S(1)}, u32[]{:S(2)}, u32[]{:S(2)}) collective-permute-start(bf16[64,256]{1,0:T(8,128)(2,1)S(1)} %get-tuple-element.37), channel_id=1, source_target_pairs={{0,16},{4,20},{8,24},{12,28},{16,0},{20,4},{24,8},{28,12},{1,17},{... | collective-permute-start | bytes 98312 | tf_op jit(solution)/shard_map/ocean_sums/ppermute | solution.py:379
  62.7 1.5 %collective-permute-start.4 = (bf16[64,256]{1,0:T(8,128)(2,1)S(1)}, bf16[64,256]{1,0:T(8,128)(2,1)S(1)}, u32[]{:S(2)}, u32[]{:S(2)}) collective-permute-start(bf16[64,256]{1,0:T(8,128)(2,1)S(1)} %get-tuple-element.38), channel_id=1, source_target_pairs={{0,8},{4,12},{8,0},{12,4},{16,24},{20,28},{24,16},{28,20},{1,9},{5... | collective-permute-start | bytes 98312 | tf_op jit(solution)/shard_map/ocean_sums/ppermute | solution.py:379
  64.2 0.6 collective-permute-start.5
  64.7 2.8 %update_of_staying_blocks.5._ = bf16[32,1024,128]{2,1,0:T(8,128)(2,1)} custom-call(s32[96]{0:T(128)S(1)} %get-tuple-element.21.order, bf16[7,4,1024,128]{3,2,1,0:T(8,128)(2,1)S(1)} %get-tuple-element.27.kept, bf16[7,1024,512]{2,1,0:T(8,128)(2,1)S(1)} %get-tuple-element.28.hidden, ...), custom_call_target="tpu_custom_call", output_to_operand_aliasing={{}: (5, {})} | custom-call | flops 1073741824 | bytes 4194304 | tf_op jit(solution)/shard_map/ocean_sums/update_of_staying_blocks/pallas_call | solution.py:473
  67.5 5.7 %all-to-all-done.1.arrived = bf16[8,1024,128]{2,1,0:T(8,128)(2,1)S(1)} async-done(((bf16[8,1024,128]{2,1,0:T(8,128)(2,1)}), bf16[8,1024,128]{2,1,0:T(8,128)(2,1)S(1)}, u32[]{:S(2)}, u32[]{:S(2)}) %all-to-all-start.1) | async-done | bytes 2097184 | tf_op jit(solution)/shard_map/all_to_all | solution.py:423
  73.2 1.5 %arrived_blocks.1.rest_3_ = bf16[32,1024,128]{2,1,0:T(8,128)(2,1)} custom-call(s32[96]{0:T(128)S(1)} %get-tuple-element.21.order, bf16[8,1024,128]{2,1,0:T(8,128)(2,1)S(1)} %all-to-all-done.1.arrived, bf16[32,1024,128]{2,1,0:T(8,128)(2,1)} %update_of_staying_blocks.5._), custom_call_target="tpu_custom_call", output_to_operand_aliasing={{}: (2, {})} | custom-call | tf_op jit(solution)/shard_map/arrived_blocks/pallas_call | solution.py:516
  74.8 0.0 collective-permute-done.3.rest_0_
  74.8 0.0 collective-permute-done.4.rest_1_
  74.8 0.0 collective-permute-done.5.rest_2_
  74.8 0.6 last_sums.1
  (2 shorter events, 0.1 us)
Async XLA Ops:
  3.1 14.3 %all-to-all-start = ((f32[8,8,128]{2,1,0:T(8,128)}), f32[8,8,128]{2,1,0:T(8,128)S(1)}, u32[]{:S(2)}, u32[]{:S(2)}) async-start(f32[8,8,128]{2,1,0:T(8,128)} %get-tuple-element.23), calls=%async_computation | async-start | bytes 65536 | tf_op jit(solution)/shard_map/all_to_all | solution.py:397
  17.4 6.0 %copy-start = (f32[8,8,128]{2,1,0:T(8,128)}, f32[8,8,128]{2,1,0:T(8,128)S(1)}, u32[]{:S(2)}) copy-start(f32[8,8,128]{2,1,0:T(8,128)S(1)} %all-to-all-done.meta_hbm) | copy-start | bytes 98308
  17.4 55.8 %all-to-all-start.1 = ((bf16[8,1024,128]{2,1,0:T(8,128)(2,1)}), bf16[8,1024,128]{2,1,0:T(8,128)(2,1)S(1)}, u32[]{:S(2)}, u32[]{:S(2)}) async-start(bf16[8,1024,128]{2,1,0:T(8,128)(2,1)} %get-tuple-element.24), calls=%async_computation.1 | async-start | bytes 4194304 | tf_op jit(solution)/shard_map/all_to_all | solution.py:423
  42.2 2.0 %collective-permute-start = (bf16[1024,256]{1,0:T(8,128)(2,1)S(1)}, bf16[1024,256]{1,0:T(8,128)(2,1)S(1)}, u32[]{:S(2)}, u32[]{:S(2)}) collective-permute-start(bf16[1024,256]{1,0:T(8,128)(2,1)S(1)} %get-tuple-element.31), channel_id=1, source_target_pairs={{0,1},{1,0},{2,3},{3,2},{4,5},{5,4},{6,7},{7,6},{8,9},{9,8},{10,11... | collective-permute-start | bytes 1572872 | tf_op jit(solution)/shard_map/ocean_sums/ppermute | solution.py:379
  44.3 8.4 %collective-permute-start.1 = (bf16[512,256]{1,0:T(8,128)(2,1)S(1)}, bf16[512,256]{1,0:T(8,128)(2,1)S(1)}, u32[]{:S(2)}, u32[]{:S(2)}) collective-permute-start(bf16[512,256]{1,0:T(8,128)(2,1)S(1)} %get-tuple-element.33), channel_id=1, source_target_pairs={{0,2},{1,3},{2,0},{3,1},{4,6},{5,7},{6,4},{7,5},{8,10},{9,11},{10,... | collective-permute-start | bytes 786440 | tf_op jit(solution)/shard_map/ocean_sums/ppermute | solution.py:379
  52.8 7.5 %collective-permute-start.2 = (bf16[256,256]{1,0:T(8,128)(2,1)S(1)}, bf16[256,256]{1,0:T(8,128)(2,1)S(1)}, u32[]{:S(2)}, u32[]{:S(2)}) collective-permute-start(bf16[256,256]{1,0:T(8,128)(2,1)S(1)} %get-tuple-element.35), channel_id=1, source_target_pairs={{0,4},{4,0},{8,12},{12,8},{16,20},{20,16},{24,28},{28,24},{1,5},{5... | collective-permute-start | bytes 393224 | tf_op jit(solution)/shard_map/ocean_sums/ppermute | solution.py:379
  60.3 14.5 %collective-permute-start.3 = (bf16[64,256]{1,0:T(8,128)(2,1)S(1)}, bf16[64,256]{1,0:T(8,128)(2,1)S(1)}, u32[]{:S(2)}, u32[]{:S(2)}) collective-permute-start(bf16[64,256]{1,0:T(8,128)(2,1)S(1)} %get-tuple-element.37), channel_id=1, source_target_pairs={{0,16},{4,20},{8,24},{12,28},{16,0},{20,4},{24,8},{28,12},{1,17},{... | collective-permute-start | bytes 98312 | tf_op jit(solution)/shard_map/ocean_sums/ppermute | solution.py:379
  62.7 12.1 %collective-permute-start.4 = (bf16[64,256]{1,0:T(8,128)(2,1)S(1)}, bf16[64,256]{1,0:T(8,128)(2,1)S(1)}, u32[]{:S(2)}, u32[]{:S(2)}) collective-permute-start(bf16[64,256]{1,0:T(8,128)(2,1)S(1)} %get-tuple-element.38), channel_id=1, source_target_pairs={{0,8},{4,12},{8,0},{12,4},{16,24},{20,28},{24,16},{28,20},{1,9},{5... | collective-permute-start | bytes 98312 | tf_op jit(solution)/shard_map/ocean_sums/ppermute | solution.py:379
  64.2 10.7 %collective-permute-start.5 = (bf16[64,256]{1,0:T(8,128)(2,1)S(1)}, bf16[64,256]{1,0:T(8,128)(2,1)S(1)}, u32[]{:S(2)}, u32[]{:S(2)}) collective-permute-start(bf16[64,256]{1,0:T(8,128)(2,1)S(1)} %get-tuple-element.39), channel_id=1, source_target_pairs={{0,24},{4,28},{8,16},{12,20},{16,8},{20,12},{24,0},{28,4},{1,25},{... | collective-permute-start | bytes 98312 | tf_op jit(solution)/shard_map/ocean_sums/ppermute | solution.py:379

commit v4 on v3

--- a/solution.py
+++ b/solution.py
@@ -88,7 +88,7 @@
         step = leaves.astype(jnp.int32)
         return kept + 1 - step, gone + step
 
-    lax.fori_loop(0, blocks, look, (jnp.int32(0), jnp.int32(0)))
+    lax.fori_loop(0, blocks, look, (jnp.int32(0), jnp.int32(0)), unroll=True)
     wait(loads[1:])
     meta[...] = jnp.zeros_like(meta)
     for k in range(move):
@@ -111,8 +111,8 @@
 
 
 def leaving_kernel(
-    order, state, w_in_hbm, w_out_hbm, w_flux_hbm, out, flux,
-    w_in, w_out, w_flux, buf_in, buf_out, hid, sem_w, sem_f, sem_in, sem_out,
+    order, state, w_in_hbm, w_out_hbm, w_flux_hbm, out, flux_hbm,
+    w_in, w_out, w_flux, flux, buf_in, buf_out, hid, sem_w, sem_f, sem_in, sem_out,
 ):
     blocks, _, cols = state.shape
     move = flux.shape[0]
@@ -127,7 +127,7 @@
     groups = move // GROUP
     load_in = row_parts(w_in_hbm, w_in, sem_w.at[0])
     load_out = row_parts(w_out_hbm, w_out, sem_w.at[1])
-    load_flux = pltpu.make_async_copy(w_flux_hbm, w_flux, sem_f)
+    load_flux = pltpu.make_async_copy(w_flux_hbm, w_flux, sem_f.at[0])
     start(arrivals_of(state, slot_of, buf_in, sem_in, 0, 0))
     start(load_in)
     load_flux.start()
@@ -151,8 +151,11 @@
         f = jnp.dot(w_flux[...], hid[...], preferred_element_type=jnp.float32)
         for j in range(GROUP):
             flux[g * GROUP + j] = f[:, j * cols : (j + 1) * cols]
+    save = pltpu.make_async_copy(flux, flux_hbm, sem_f.at[1])
+    save.start()
     for g in range(max(groups - 2, 0), groups):
         wait(departures(buf_out, out, row_of, sem_out, g, g % 2))
+    save.wait()
 
 
 def staying_kernel(
@@ -403,16 +406,17 @@
             leaving_kernel,
             out_shape=(pltpu.HBM((nwide, depth, cols), bf16), pltpu.HBM((move, nflux, cols), f32)),
             in_specs=[SMEM, HBM, HBM, HBM, HBM],
-            out_specs=(HBM, VMEM),
+            out_specs=(HBM, HBM),
             scratch_shapes=[
                 pltpu.VMEM((inner, depth), bf16),
                 pltpu.VMEM((depth, inner), bf16),
                 pltpu.VMEM((nflux, inner), bf16),
+                pltpu.VMEM((move, nflux, cols), f32),
                 pltpu.VMEM((2, GROUP, depth, cols), bf16),
                 pltpu.VMEM((2, GROUP, depth, cols), bf16),
                 pltpu.VMEM((inner, side), bf16),
                 dma((2, parts)),
-                dma,
+                dma((2,)),
                 dma((2, GROUP)),
                 dma((2, GROUP)),
             ],

time: 75.8 us -> 75 us (0.989)
  Pallas kernels: 44.2 us -> 43.3 us
  transfers between devices with their start and end apart: 8 -> 8, of which waited for: 3 -> 4; matrix products, arithmetic and copies ran while one was open for 0% -> 0% of each run, Pallas kernels for 54% -> 54%
where the time goes in v4:
time: 75 us; the launch traced here: 74.6 us
  Pallas kernels  43.3 us (58%)
  starting transfers between devices  21.2 us (28%)
  waiting for transfers between devices  9.41 us (13%)
  between operations  0.75 us (1%)
    pallas_call x1, Pallas kernels, per_device(): pl.pallas_call(functools.partial(staying_kernel, devices, nnarrow), out_s...  18.8 us
    pallas_call x3, Pallas kernels, update(): pl.pallas_call(functools.partial(update_kernel, done, upto), out_shape=sh...  13.5 us
    ppermute x6, starting transfers between devices, swap(): lax.ppermute(x, axis, [(i, i ^ bit) for i in range(lax.axis_size(axis))])  8.17 us
    all_to_all x1, starting transfers between devices, per_device(): meta = lax.all_to_all(meta, 'wide', split_axis=0, concat_axis=0, tiled=True)  7.29 us
    pallas_call x1, Pallas kernels, per_device(): pl.pallas_call(leaving_kernel, out_shape=(pltpu.HBM((nwide, depth, cols),...  6.35 us
    all_to_all x1, waiting for transfers between devices, per_device(): lax.all_to_all(outgoing, 'wide', split_axis=0, concat_axis=0, tiled=True)  5.71 us
    all_to_all x1, starting transfers between devices, per_device(): lax.all_to_all(outgoing, 'wide', split_axis=0, concat_axis=0, tiled=True)  5.69 us
    ppermute x6, waiting for transfers between devices, swap(): lax.ppermute(x, axis, [(i, i ^ bit) for i in range(lax.axis_size(axis))])  3.37 us
  transfers between devices with their start and end apart: 8, of which 4 were waited for; matrix products, arithmetic and copies ran while one was open for 0% of the time, Pallas kernels for 54%

profile of v4, /device:TPU:0, one launch (start us, length us, event | category | flops | bytes accessed | tf_op | source)
XLA Modules:
  0.0 74.6 jit_solution(1631073434826362296)
XLA Ops:
  0.6 2.2 %order_of_blocks.1 = (s32[96]{0:T(128)S(1)}, f32[8,8,128]{2,1,0:T(8,128)}) custom-call(s32[1024]{0:T(1024)} %table_hbm.1, s32[32,128]{1,0:T(8,128)} %bitcast.3, s32[32,128]{1,0:T(8,128)} %bitcast.5, f32[32,128]{1,0:T(8,128)} %bitcast.7), custom_call_target="tpu_custom_call" | custom-call | tf_op jit(solution)/shard_map/order_of_blocks/pallas_call | solution.py:385
  2.9 7.3 %all-to-all-start = ((f32[8,8,128]{2,1,0:T(8,128)}), f32[8,8,128]{2,1,0:T(8,128)S(1)}, u32[]{:S(2)}, u32[]{:S(2)}) async-start(f32[8,8,128]{2,1,0:T(8,128)} %get-tuple-element.23), calls=%async_computation | async-start | bytes 65536 | tf_op jit(solution)/shard_map/all_to_all | solution.py:400
  10.2 6.3 %leaving_blocks.1 = (bf16[8,1024,128]{2,1,0:T(8,128)(2,1)}, f32[4,32,128]{2,1,0:T(8,128)}) custom-call(s32[96]{0:T(128)S(1)} %get-tuple-element.21.order, bf16[32,1024,128]{2,1,0:T(8,128)(2,1)} %state.3, bf16[1024,1024]{1,0:T(8,128)(2,1)} %w_in_hbm.3, bf16[1024,1024]{1,0:T(8,128)(2,1)} %w_out_hbm.3, bf16[32,1024]{1,0:T(8,128)(2,1)} %w_flux_hbm.3), custom_call_target="tpu_custom_call" | custom-call | flops 2147483648 | bytes 6291456 | tf_op jit(solution)/shard_map/leaving_blocks/pallas_call | solution.py:405
  16.5 0.3 all-to-all-done.meta_hbm
  16.8 0.0 copy-start
  16.9 5.7 %all-to-all-start.1 = ((bf16[8,1024,128]{2,1,0:T(8,128)(2,1)}), bf16[8,1024,128]{2,1,0:T(8,128)(2,1)S(1)}, u32[]{:S(2)}, u32[]{:S(2)}) async-start(bf16[8,1024,128]{2,1,0:T(8,128)(2,1)} %get-tuple-element.24), calls=%async_computation.1 | async-start | bytes 4194304 | tf_op jit(solution)/shard_map/all_to_all | solution.py:427
  22.5 0.0 copy-done
  22.5 18.8 %staying_blocks_and_cell_sums.1 = (bf16[7,1024,512]{2,1,0:T(8,128)(2,1)S(1)}, bf16[7,4,1024,128]{3,2,1,0:T(8,128)(2,1)S(1)}, bf16[1024,1024]{1,0:T(8,128)(2,1)S(...) custom-call(s32[96]{0:T(128)S(1)} %get-tuple-element.21.order, bf16[32,1024,128]{2,1,0:T(8,128)(2,1)} %state.3, ...), custom_call_target="tpu_custom_call" | custom-call | flops 11811160064 | bytes 11534336 | tf_op jit(solution)/shard_map/staying_blocks_and_cell_sums/pallas_call | solution.py:431
  41.4 0.1 collective-permute-start
  41.5 1.9 %collective-permute-done.came = bf16[1024,256]{1,0:T(8,128)(2,1)S(1)} collective-permute-done((bf16[1024,256]{1,0:T(8,128)(2,1)S(1)}, bf16[1024,256]{1,0:T(8,128)(2,1)S(1)}, u32[]{:S(2)}, u32[]{:S(2)}) %collective-permute-start) | collective-permute-done | bytes 524320 | tf_op jit(solution)/shard_map/ocean_sums/ppermute | solution.py:382
  43.4 0.1 ocean_sums.3
  43.5 1.6 %collective-permute-start.1 = (bf16[512,256]{1,0:T(8,128)(2,1)S(1)}, bf16[512,256]{1,0:T(8,128)(2,1)S(1)}, u32[]{:S(2)}, u32[]{:S(2)}) collective-permute-start(bf16[512,256]{1,0:T(8,128)(2,1)S(1)} %get-tuple-element.33), channel_id=1, source_target_pairs={{0,2},{1,3},{2,0},{3,1},{4,6},{5,7},{6,4},{7,5},{8,10},{9,11},{10,... | collective-permute-start | bytes 786440 | tf_op jit(solution)/shard_map/ocean_sums/ppermute | solution.py:382
  45.0 5.4 %update_of_staying_blocks.3.rest_1_ = bf16[32,1024,128]{2,1,0:T(8,128)(2,1)} custom-call(s32[96]{0:T(128)S(1)} %get-tuple-element.21.order, bf16[7,4,1024,128]{3,2,1,0:T(8,128)(2,1)S(1)} %get-tuple-element.27.kept, bf16[7,1024,512]{2,1,0:T(8,128)(2,1)S(1)} %get-tuple-element.28.hidden, bf16[1024,1024]{1,0:T(8,128)(2,1)S(1)} %get-tuple-element.29.w_out, ...), custom_call_target="tpu_custom_call" | custom-call | flops 3221225472 | bytes 8388608 | tf_op jit(solution)/shard_map/ocean_sums/update_of_staying_blocks/pallas_call | solution.py:477
  50.4 1.5 %collective-permute-done.1.came = bf16[512,256]{1,0:T(8,128)(2,1)S(1)} collective-permute-done((bf16[512,256]{1,0:T(8,128)(2,1)S(1)}, bf16[512,256]{1,0:T(8,128)(2,1)S(1)}, u32[]{:S(2)}, u32[]{:S(2)}) %collective-permute-start.1) | collective-permute-done | bytes 262176 | tf_op jit(solution)/shard_map/ocean_sums/ppermute | solution.py:382
  51.9 2.1 %collective-permute-start.2 = (bf16[256,256]{1,0:T(8,128)(2,1)S(1)}, bf16[256,256]{1,0:T(8,128)(2,1)S(1)}, u32[]{:S(2)}, u32[]{:S(2)}) collective-permute-start(bf16[256,256]{1,0:T(8,128)(2,1)S(1)} %get-tuple-element.35), channel_id=1, source_target_pairs={{0,4},{4,0},{8,12},{12,8},{16,20},{20,16},{24,28},{28,24},{1,5},{5... | collective-permute-start | bytes 393224 | tf_op jit(solution)/shard_map/ocean_sums/ppermute | solution.py:382
  54.0 5.4 %update_of_staying_blocks.4.rest_1_ = bf16[32,1024,128]{2,1,0:T(8,128)(2,1)} custom-call(s32[96]{0:T(128)S(1)} %get-tuple-element.21.order, bf16[7,4,1024,128]{3,2,1,0:T(8,128)(2,1)S(1)} %get-tuple-element.27.kept, bf16[7,1024,512]{2,1,0:T(8,128)(2,1)S(1)} %get-tuple-element.28.hidden, ...), custom_call_target="tpu_custom_call", output_to_operand_aliasing={{}: (5, {})} | custom-call | flops 3221225472 | bytes 8388608 | tf_op jit(solution)/shard_map/ocean_sums/update_of_staying_blocks/pallas_call | solution.py:477
  59.4 0.0 collective-permute-done.2.came
  59.4 2.4 %collective-permute-start.3 = (bf16[64,256]{1,0:T(8,128)(2,1)S(1)}, bf16[64,256]{1,0:T(8,128)(2,1)S(1)}, u32[]{:S(2)}, u32[]{:S(2)}) collective-permute-start(bf16[64,256]{1,0:T(8,128)(2,1)S(1)} %get-tuple-element.37), channel_id=1, source_target_pairs={{0,16},{4,20},{8,24},{12,28},{16,0},{20,4},{24,8},{28,12},{1,17},{... | collective-permute-start | bytes 98312 | tf_op jit(solution)/shard_map/ocean_sums/ppermute | solution.py:382
  61.9 1.5 %collective-permute-start.4 = (bf16[64,256]{1,0:T(8,128)(2,1)S(1)}, bf16[64,256]{1,0:T(8,128)(2,1)S(1)}, u32[]{:S(2)}, u32[]{:S(2)}) collective-permute-start(bf16[64,256]{1,0:T(8,128)(2,1)S(1)} %get-tuple-element.38), channel_id=1, source_target_pairs={{0,8},{4,12},{8,0},{12,4},{16,24},{20,28},{24,16},{28,20},{1,9},{5... | collective-permute-start | bytes 98312 | tf_op jit(solution)/shard_map/ocean_sums/ppermute | solution.py:382
  63.3 0.6 collective-permute-start.5
  63.9 2.8 %update_of_staying_blocks.5._ = bf16[32,1024,128]{2,1,0:T(8,128)(2,1)} custom-call(s32[96]{0:T(128)S(1)} %get-tuple-element.21.order, bf16[7,4,1024,128]{3,2,1,0:T(8,128)(2,1)S(1)} %get-tuple-element.27.kept, bf16[7,1024,512]{2,1,0:T(8,128)(2,1)S(1)} %get-tuple-element.28.hidden, ...), custom_call_target="tpu_custom_call", output_to_operand_aliasing={{}: (5, {})} | custom-call | flops 1073741824 | bytes 4194304 | tf_op jit(solution)/shard_map/ocean_sums/update_of_staying_blocks/pallas_call | solution.py:477
  66.7 5.7 %all-to-all-done.1.arrived = bf16[8,1024,128]{2,1,0:T(8,128)(2,1)S(1)} async-done(((bf16[8,1024,128]{2,1,0:T(8,128)(2,1)}), bf16[8,1024,128]{2,1,0:T(8,128)(2,1)S(1)}, u32[]{:S(2)}, u32[]{:S(2)}) %all-to-all-start.1) | async-done | bytes 2097184 | tf_op jit(solution)/shard_map/all_to_all | solution.py:427
  72.4 1.5 %arrived_blocks.1.rest_3_ = bf16[32,1024,128]{2,1,0:T(8,128)(2,1)} custom-call(s32[96]{0:T(128)S(1)} %get-tuple-element.21.order, bf16[8,1024,128]{2,1,0:T(8,128)(2,1)S(1)} %all-to-all-done.1.arrived, bf16[32,1024,128]{2,1,0:T(8,128)(2,1)} %update_of_staying_blocks.5._), custom_call_target="tpu_custom_call", output_to_operand_aliasing={{}: (2, {})} | custom-call | tf_op jit(solution)/shard_map/arrived_blocks/pallas_call | solution.py:520
  73.9 0.0 collective-permute-done.3.rest_0_
  73.9 0.0 collective-permute-done.4.rest_1_
  73.9 0.0 collective-permute-done.5.rest_2_
  74.0 0.6 last_sums.1
  (2 shorter events, 0.1 us)
Async XLA Ops:
  2.9 14.0 %all-to-all-start = ((f32[8,8,128]{2,1,0:T(8,128)}), f32[8,8,128]{2,1,0:T(8,128)S(1)}, u32[]{:S(2)}, u32[]{:S(2)}) async-start(f32[8,8,128]{2,1,0:T(8,128)} %get-tuple-element.23), calls=%async_computation | async-start | bytes 65536 | tf_op jit(solution)/shard_map/all_to_all | solution.py:400
  16.8 5.7 %copy-start = (f32[8,8,128]{2,1,0:T(8,128)}, f32[8,8,128]{2,1,0:T(8,128)S(1)}, u32[]{:S(2)}) copy-start(f32[8,8,128]{2,1,0:T(8,128)S(1)} %all-to-all-done.meta_hbm) | copy-start | bytes 98308
  16.9 55.5 %all-to-all-start.1 = ((bf16[8,1024,128]{2,1,0:T(8,128)(2,1)}), bf16[8,1024,128]{2,1,0:T(8,128)(2,1)S(1)}, u32[]{:S(2)}, u32[]{:S(2)}) async-start(bf16[8,1024,128]{2,1,0:T(8,128)(2,1)} %get-tuple-element.24), calls=%async_computation.1 | async-start | bytes 4194304 | tf_op jit(solution)/shard_map/all_to_all | solution.py:427
  41.4 2.0 %collective-permute-start = (bf16[1024,256]{1,0:T(8,128)(2,1)S(1)}, bf16[1024,256]{1,0:T(8,128)(2,1)S(1)}, u32[]{:S(2)}, u32[]{:S(2)}) collective-permute-start(bf16[1024,256]{1,0:T(8,128)(2,1)S(1)} %get-tuple-element.31), channel_id=1, source_target_pairs={{0,1},{1,0},{2,3},{3,2},{4,5},{5,4},{6,7},{7,6},{8,9},{9,8},{10,11... | collective-permute-start | bytes 1572872 | tf_op jit(solution)/shard_map/ocean_sums/ppermute | solution.py:382
  43.5 8.4 %collective-permute-start.1 = (bf16[512,256]{1,0:T(8,128)(2,1)S(1)}, bf16[512,256]{1,0:T(8,128)(2,1)S(1)}, u32[]{:S(2)}, u32[]{:S(2)}) collective-permute-start(bf16[512,256]{1,0:T(8,128)(2,1)S(1)} %get-tuple-element.33), channel_id=1, source_target_pairs={{0,2},{1,3},{2,0},{3,1},{4,6},{5,7},{6,4},{7,5},{8,10},{9,11},{10,... | collective-permute-start | bytes 786440 | tf_op jit(solution)/shard_map/ocean_sums/ppermute | solution.py:382
  51.9 7.5 %collective-permute-start.2 = (bf16[256,256]{1,0:T(8,128)(2,1)S(1)}, bf16[256,256]{1,0:T(8,128)(2,1)S(1)}, u32[]{:S(2)}, u32[]{:S(2)}) collective-permute-start(bf16[256,256]{1,0:T(8,128)(2,1)S(1)} %get-tuple-element.35), channel_id=1, source_target_pairs={{0,4},{4,0},{8,12},{12,8},{16,20},{20,16},{24,28},{28,24},{1,5},{5... | collective-permute-start | bytes 393224 | tf_op jit(solution)/shard_map/ocean_sums/ppermute | solution.py:382
  59.4 14.5 %collective-permute-start.3 = (bf16[64,256]{1,0:T(8,128)(2,1)S(1)}, bf16[64,256]{1,0:T(8,128)(2,1)S(1)}, u32[]{:S(2)}, u32[]{:S(2)}) collective-permute-start(bf16[64,256]{1,0:T(8,128)(2,1)S(1)} %get-tuple-element.37), channel_id=1, source_target_pairs={{0,16},{4,20},{8,24},{12,28},{16,0},{20,4},{24,8},{28,12},{1,17},{... | collective-permute-start | bytes 98312 | tf_op jit(solution)/shard_map/ocean_sums/ppermute | solution.py:382
  61.9 12.1 %collective-permute-start.4 = (bf16[64,256]{1,0:T(8,128)(2,1)S(1)}, bf16[64,256]{1,0:T(8,128)(2,1)S(1)}, u32[]{:S(2)}, u32[]{:S(2)}) collective-permute-start(bf16[64,256]{1,0:T(8,128)(2,1)S(1)} %get-tuple-element.38), channel_id=1, source_target_pairs={{0,8},{4,12},{8,0},{12,4},{16,24},{20,28},{24,16},{28,20},{1,9},{5... | collective-permute-start | bytes 98312 | tf_op jit(solution)/shard_map/ocean_sums/ppermute | solution.py:382
  63.3 10.6 %collective-permute-start.5 = (bf16[64,256]{1,0:T(8,128)(2,1)S(1)}, bf16[64,256]{1,0:T(8,128)(2,1)S(1)}, u32[]{:S(2)}, u32[]{:S(2)}) collective-permute-start(bf16[64,256]{1,0:T(8,128)(2,1)S(1)} %get-tuple-element.39), channel_id=1, source_target_pairs={{0,24},{4,28},{8,16},{12,20},{16,8},{20,12},{24,0},{28,4},{1,25},{... | collective-permute-start | bytes 98312 | tf_op jit(solution)/shard_map/ocean_sums/ppermute | solution.py:382

commit v5 on v4

--- a/solution.py
+++ b/solution.py
@@ -66,8 +66,8 @@
 
 
 def order_kernel(
-    nwide, nnarrow, move, table_hbm, owner_hbm, slot_hbm, weight_hbm, order, meta_hbm,
-    table, owner, slot, weight, meta, sem,
+    nwide, nnarrow, move, table_hbm, owner_hbm, slot_hbm, weight_hbm, order_hbm, meta_hbm,
+    order, table, owner, slot, weight, meta, sem,
 ):
     blocks = owner.shape[0]
     stay = blocks - move
@@ -89,6 +89,8 @@
         return kept + 1 - step, gone + step
 
     lax.fori_loop(0, blocks, look, (jnp.int32(0), jnp.int32(0)), unroll=True)
+    save_order = pltpu.make_async_copy(order, order_hbm, sem.at[len(pairs) + 1])
+    save_order.start()
     wait(loads[1:])
     meta[...] = jnp.zeros_like(meta)
     for k in range(move):
@@ -100,6 +102,7 @@
     save = pltpu.make_async_copy(meta, meta_hbm, sem.at[len(pairs)])
     save.start()
     save.wait()
+    save_order.wait()
 
 
 def row_parts(src, dst, sem):
@@ -111,8 +114,8 @@
 
 
 def leaving_kernel(
-    order, state, w_in_hbm, w_out_hbm, w_flux_hbm, out, flux_hbm,
-    w_in, w_out, w_flux, flux, buf_in, buf_out, hid, sem_w, sem_f, sem_in, sem_out,
+    order_hbm, state, w_in_hbm, w_out_hbm, w_flux_hbm, out, flux_hbm,
+    w_in, w_out, w_flux, flux, order, buf_in, buf_out, hid, sem_w, sem_f, sem_in, sem_out,
 ):
     blocks, _, cols = state.shape
     move = flux.shape[0]
@@ -128,8 +131,11 @@
     load_in = row_parts(w_in_hbm, w_in, sem_w.at[0])
     load_out = row_parts(w_out_hbm, w_out, sem_w.at[1])
     load_flux = pltpu.make_async_copy(w_flux_hbm, w_flux, sem_f.at[0])
+    load_order = pltpu.make_async_copy(order_hbm, order, sem_f.at[2])
+    load_order.start()
+    start(load_in)
+    load_order.wait()
     start(arrivals_of(state, slot_of, buf_in, sem_in, 0, 0))
-    start(load_in)
     load_flux.start()
     for g in range(groups):
         b = g % 2
@@ -384,16 +390,17 @@
     with jax.named_scope("order_of_blocks"):
         order, meta = pl.pallas_call(
             functools.partial(order_kernel, nwide, nnarrow, move),
-            out_shape=(shape((3 * blocks,), i32), pltpu.HBM((nwide, 8, cols), f32)),
+            out_shape=(pltpu.HBM((3 * blocks,), i32), pltpu.HBM((nwide, 8, cols), f32)),
             in_specs=[HBM] * 4,
-            out_specs=(SMEM, HBM),
+            out_specs=(HBM, HBM),
             scratch_shapes=[
+                pltpu.SMEM((3 * blocks,), i32),
                 pltpu.SMEM(group_of.shape, i32),
                 pltpu.VMEM((blocks, cols), i32),
                 pltpu.VMEM((blocks, cols), i32),
                 pltpu.VMEM((blocks, cols), f32),
                 pltpu.VMEM((nwide, 8, cols), f32),
-                dma((5,)),
+                dma((6,)),
             ],
             compiler_params=params,
         )(in_hbm(group_of), in_hbm(owner), in_hbm(slot), in_hbm(weight))
@@ -405,24 +412,25 @@
         outgoing, flux_away = pl.pallas_call(
             leaving_kernel,
             out_shape=(pltpu.HBM((nwide, depth, cols), bf16), pltpu.HBM((move, nflux, cols), f32)),
-            in_specs=[SMEM, HBM, HBM, HBM, HBM],
+            in_specs=[HBM] * 5,
             out_specs=(HBM, HBM),
             scratch_shapes=[
                 pltpu.VMEM((inner, depth), bf16),
                 pltpu.VMEM((depth, inner), bf16),
                 pltpu.VMEM((nflux, inner), bf16),
                 pltpu.VMEM((move, nflux, cols), f32),
+                pltpu.SMEM((3 * blocks,), i32),
                 pltpu.VMEM((2, GROUP, depth, cols), bf16),
                 pltpu.VMEM((2, GROUP, depth, cols), bf16),
                 pltpu.VMEM((inner, side), bf16),
                 dma((2, parts)),
-                dma((2,)),
+                dma((3,)),
                 dma((2, GROUP)),
                 dma((2, GROUP)),
             ],
             compiler_params=params,
             cost_estimate=cost(move, 2),
-        )(order, in_hbm(state), in_hbm(w_in), in_hbm(w_out), in_hbm(w_flux))
+        )(in_hbm(order), in_hbm(state), in_hbm(w_in), in_hbm(w_out), in_hbm(w_flux))
     outgoing, meta = lax.optimization_barrier((outgoing, meta))
     arrived = lax.all_to_all(outgoing, "wide", split_axis=0, concat_axis=0, tiled=True)
 

time: 75 us -> 74.2 us (0.989)
  Pallas kernels: 43.3 us -> 42.5 us
where the time goes in v5:
time: 74.2 us; the launch traced here: 73.8 us
  Pallas kernels  42.5 us (57%)
  starting transfers between devices  21 us (28%)
  waiting for transfers between devices  9.58 us (13%)
  between operations  0.76 us (1%)
    pallas_call x1, Pallas kernels, per_device(): pl.pallas_call(functools.partial(staying_kernel, devices, nnarrow), out_s...  18.8 us
    pallas_call x3, Pallas kernels, update(): pl.pallas_call(functools.partial(update_kernel, done, upto), out_shape=sh...  13.5 us
    ppermute x6, starting transfers between devices, swap(): lax.ppermute(x, axis, [(i, i ^ bit) for i in range(lax.axis_size(axis))])  8.17 us
    all_to_all x1, starting transfers between devices, per_device(): meta = lax.all_to_all(meta, 'wide', split_axis=0, concat_axis=0, tiled=True)  7.29 us
    pallas_call x1, Pallas kernels, per_device(): pl.pallas_call(leaving_kernel, out_shape=(pltpu.HBM((nwide, depth, cols),...  6.14 us
    all_to_all x1, waiting for transfers between devices, per_device(): lax.all_to_all(outgoing, 'wide', split_axis=0, concat_axis=0, tiled=True)  5.68 us
    all_to_all x1, starting transfers between devices, per_device(): lax.all_to_all(outgoing, 'wide', split_axis=0, concat_axis=0, tiled=True)  5.51 us
    ppermute x6, waiting for transfers between devices, swap(): lax.ppermute(x, axis, [(i, i ^ bit) for i in range(lax.axis_size(axis))])  3.37 us
  transfers between devices with their start and end apart: 8, of which 4 were waited for; matrix products, arithmetic and copies ran while one was open for 0% of the time, Pallas kernels for 54%

profile of v5, /device:TPU:0, one launch (start us, length us, event | category | flops | bytes accessed | tf_op | source)
XLA Modules:
  0.0 73.8 jit_solution(12138136333341096091)
XLA Ops:
  0.6 1.7 %order_of_blocks.1 = (s32[96]{0:T(128)}, f32[8,8,128]{2,1,0:T(8,128)}) custom-call(s32[1024]{0:T(1024)} %table_hbm.1, s32[32,128]{1,0:T(8,128)} %bitcast.3, s32[32,128]{1,0:T(8,128)} %bitcast.5, f32[32,128]{1,0:T(8,128)} %bitcast.7), custom_call_target="tpu_custom_call" | custom-call | tf_op jit(solution)/shard_map/order_of_blocks/pallas_call | solution.py:391
  2.3 7.3 %all-to-all-start = ((f32[8,8,128]{2,1,0:T(8,128)}), f32[8,8,128]{2,1,0:T(8,128)S(1)}, u32[]{:S(2)}, u32[]{:S(2)}) async-start(f32[8,8,128]{2,1,0:T(8,128)} %get-tuple-element.23), calls=%async_computation | async-start | bytes 65536 | tf_op jit(solution)/shard_map/all_to_all | solution.py:407
  9.6 0.0 copy-start
  9.6 6.1 %leaving_blocks.1 = (bf16[8,1024,128]{2,1,0:T(8,128)(2,1)}, f32[4,32,128]{2,1,0:T(8,128)}) custom-call(s32[96]{0:T(128)} %get-tuple-element.21.order_hbm.order, bf16[32,1024,128]{2,1,0:T(8,128)(2,1)} %state.3, bf16[1024,1024]{1,0:T(8,128)(2,1)} %w_in_hbm.3, bf16[1024,1024]{1,0:T(8,128)(2,1)} %w_out_hbm.3, bf16[32,1024]{1,0:T(8,128)(2,1)} %w_flux_hbm.3), custom_call_target="tpu_custom_call" | custom-call | flops 2147483648 | bytes 6291456 | tf_op jit(solution)/shard_map/leaving_blocks/pallas_call | solution.py:412
  15.7 0.5 all-to-all-done.meta_hbm
  16.3 0.0 copy-start.1
  16.3 5.5 %all-to-all-start.1 = ((bf16[8,1024,128]{2,1,0:T(8,128)(2,1)}), bf16[8,1024,128]{2,1,0:T(8,128)(2,1)S(1)}, u32[]{:S(2)}, u32[]{:S(2)}) async-start(bf16[8,1024,128]{2,1,0:T(8,128)(2,1)} %get-tuple-element.24), calls=%async_computation.1 | async-start | bytes 4194304 | tf_op jit(solution)/shard_map/all_to_all | solution.py:435
  21.8 0.0 copy-done.1
  21.8 0.0 copy-done
  21.8 18.8 %staying_blocks_and_cell_sums.1 = (bf16[7,1024,512]{2,1,0:T(8,128)(2,1)S(1)}, bf16[7,4,1024,128]{3,2,1,0:T(8,128)(2,1)S(1)}, bf16[1024,1024]{1,0:T(8,128)(2,1)S(...) custom-call(s32[96]{0:T(128)S(1)} %copy-done, bf16[32,1024,128]{2,1,0:T(8,128)(2,1)} %state.3, ...), custom_call_target="tpu_custom_call" | custom-call | flops 11811160064 | bytes 11534336 | tf_op jit(solution)/shard_map/staying_blocks_and_cell_sums/pallas_call | solution.py:439
  40.6 0.1 collective-permute-start
  40.7 1.9 %collective-permute-done.came = bf16[1024,256]{1,0:T(8,128)(2,1)S(1)} collective-permute-done((bf16[1024,256]{1,0:T(8,128)(2,1)S(1)}, bf16[1024,256]{1,0:T(8,128)(2,1)S(1)}, u32[]{:S(2)}, u32[]{:S(2)}) %collective-permute-start) | collective-permute-done | bytes 524320 | tf_op jit(solution)/shard_map/ocean_sums/ppermute | solution.py:388
  42.6 0.1 ocean_sums.3
  42.7 1.6 %collective-permute-start.1 = (bf16[512,256]{1,0:T(8,128)(2,1)S(1)}, bf16[512,256]{1,0:T(8,128)(2,1)S(1)}, u32[]{:S(2)}, u32[]{:S(2)}) collective-permute-start(bf16[512,256]{1,0:T(8,128)(2,1)S(1)} %get-tuple-element.33), channel_id=1, source_target_pairs={{0,2},{1,3},{2,0},{3,1},{4,6},{5,7},{6,4},{7,5},{8,10},{9,11},{10,... | collective-permute-start | bytes 786440 | tf_op jit(solution)/shard_map/ocean_sums/ppermute | solution.py:388
  44.3 5.4 %update_of_staying_blocks.3.rest_1_ = bf16[32,1024,128]{2,1,0:T(8,128)(2,1)} custom-call(s32[96]{0:T(128)S(1)} %copy-done, bf16[7,4,1024,128]{3,2,1,0:T(8,128)(2,1)S(1)} %get-tuple-element.27.kept, bf16[7,1024,512]{2,1,0:T(8,128)(2,1)S(1)} %get-tuple-element.28.hidden, bf16[1024,1024]{1,0:T(8,128)(2,1)S(1)} %get-tuple-element.29.w_out, ...), custom_call_target="tpu_custom_call" | custom-call | flops 3221225472 | bytes 8388608 | tf_op jit(solution)/shard_map/ocean_sums/update_of_staying_blocks/pallas_call | solution.py:485
  49.7 1.5 %collective-permute-done.1.came = bf16[512,256]{1,0:T(8,128)(2,1)S(1)} collective-permute-done((bf16[512,256]{1,0:T(8,128)(2,1)S(1)}, bf16[512,256]{1,0:T(8,128)(2,1)S(1)}, u32[]{:S(2)}, u32[]{:S(2)}) %collective-permute-start.1) | collective-permute-done | bytes 262176 | tf_op jit(solution)/shard_map/ocean_sums/ppermute | solution.py:388
  51.2 2.1 %collective-permute-start.2 = (bf16[256,256]{1,0:T(8,128)(2,1)S(1)}, bf16[256,256]{1,0:T(8,128)(2,1)S(1)}, u32[]{:S(2)}, u32[]{:S(2)}) collective-permute-start(bf16[256,256]{1,0:T(8,128)(2,1)S(1)} %get-tuple-element.35), channel_id=1, source_target_pairs={{0,4},{4,0},{8,12},{12,8},{16,20},{20,16},{24,28},{28,24},{1,5},{5... | collective-permute-start | bytes 393224 | tf_op jit(solution)/shard_map/ocean_sums/ppermute | solution.py:388
  53.3 5.4 %update_of_staying_blocks.4.rest_1_ = bf16[32,1024,128]{2,1,0:T(8,128)(2,1)} custom-call(s32[96]{0:T(128)S(1)} %copy-done, bf16[7,4,1024,128]{3,2,1,0:T(8,128)(2,1)S(1)} %get-tuple-element.27.kept, bf16[7,1024,512]{2,1,0:T(8,128)(2,1)S(1)} %get-tuple-element.28.hidden, ...), custom_call_target="tpu_custom_call", output_to_operand_aliasing={{}: (5, {})} | custom-call | flops 3221225472 | bytes 8388608 | tf_op jit(solution)/shard_map/ocean_sums/update_of_staying_blocks/pallas_call | solution.py:485
  58.6 0.0 collective-permute-done.2.came
  58.7 2.4 %collective-permute-start.3 = (bf16[64,256]{1,0:T(8,128)(2,1)S(1)}, bf16[64,256]{1,0:T(8,128)(2,1)S(1)}, u32[]{:S(2)}, u32[]{:S(2)}) collective-permute-start(bf16[64,256]{1,0:T(8,128)(2,1)S(1)} %get-tuple-element.37), channel_id=1, source_target_pairs={{0,16},{4,20},{8,24},{12,28},{16,0},{20,4},{24,8},{28,12},{1,17},{... | collective-permute-start | bytes 98312 | tf_op jit(solution)/shard_map/ocean_sums/ppermute | solution.py:388
  61.1 1.5 %collective-permute-start.4 = (bf16[64,256]{1,0:T(8,128)(2,1)S(1)}, bf16[64,256]{1,0:T(8,128)(2,1)S(1)}, u32[]{:S(2)}, u32[]{:S(2)}) collective-permute-start(bf16[64,256]{1,0:T(8,128)(2,1)S(1)} %get-tuple-element.38), channel_id=1, source_target_pairs={{0,8},{4,12},{8,0},{12,4},{16,24},{20,28},{24,16},{28,20},{1,9},{5... | collective-permute-start | bytes 98312 | tf_op jit(solution)/shard_map/ocean_sums/ppermute | solution.py:388
  62.6 0.6 collective-permute-start.5
  63.1 2.8 %update_of_staying_blocks.5._ = bf16[32,1024,128]{2,1,0:T(8,128)(2,1)} custom-call(s32[96]{0:T(128)S(1)} %copy-done, bf16[7,4,1024,128]{3,2,1,0:T(8,128)(2,1)S(1)} %get-tuple-element.27.kept, bf16[7,1024,512]{2,1,0:T(8,128)(2,1)S(1)} %get-tuple-element.28.hidden, bf16[1024,1024]{1,0:T(8,128)(2,1)S(1)} %get-tuple-element.29.w_out, ...), custom_call_target="tpu_custom_call", output_to_operand_aliasing={{}: (5, {})} | custom-call | flops 1073741824 | bytes 4194304 | tf_op jit(solution)/shard_map/ocean_sums/update_of_staying_blocks/pallas_call | solution.py:485
  65.9 5.7 %all-to-all-done.1.arrived = bf16[8,1024,128]{2,1,0:T(8,128)(2,1)S(1)} async-done(((bf16[8,1024,128]{2,1,0:T(8,128)(2,1)}), bf16[8,1024,128]{2,1,0:T(8,128)(2,1)S(1)}, u32[]{:S(2)}, u32[]{:S(2)}) %all-to-all-start.1) | async-done | bytes 2097184 | tf_op jit(solution)/shard_map/all_to_all | solution.py:435
  71.6 1.5 %arrived_blocks.1.rest_3_ = bf16[32,1024,128]{2,1,0:T(8,128)(2,1)} custom-call(s32[96]{0:T(128)S(1)} %copy-done, bf16[8,1024,128]{2,1,0:T(8,128)(2,1)S(1)} %all-to-all-done.1.arrived, bf16[32,1024,128]{2,1,0:T(8,128)(2,1)} %update_of_staying_blocks.5._), custom_call_target="tpu_custom_call", output_to_operand_aliasing={{}: (2, {})} | custom-call | tf_op jit(solution)/shard_map/arrived_blocks/pallas_call | solution.py:528
  73.1 0.0 collective-permute-done.3.rest_0_
  73.2 0.0 collective-permute-done.4.rest_1_
  73.2 0.0 collective-permute-done.5.rest_2_
  73.2 0.6 last_sums.1
  (2 shorter events, 0.1 us)
Async XLA Ops:
  2.3 14.0 %all-to-all-start = ((f32[8,8,128]{2,1,0:T(8,128)}), f32[8,8,128]{2,1,0:T(8,128)S(1)}, u32[]{:S(2)}, u32[]{:S(2)}) async-start(f32[8,8,128]{2,1,0:T(8,128)} %get-tuple-element.23), calls=%async_computation | async-start | bytes 65536 | tf_op jit(solution)/shard_map/all_to_all | solution.py:407
  9.6 12.2 %copy-start = (s32[96]{0:T(128)S(1)}, s32[96]{0:T(128)}, u32[]{:S(2)}) copy-start(s32[96]{0:T(128)} %get-tuple-element.21.order_hbm.order) | copy-start | bytes 1156
  16.3 5.5 %copy-start.1 = (f32[8,8,128]{2,1,0:T(8,128)}, f32[8,8,128]{2,1,0:T(8,128)S(1)}, u32[]{:S(2)}) copy-start(f32[8,8,128]{2,1,0:T(8,128)S(1)} %all-to-all-done.meta_hbm) | copy-start | bytes 98308
  16.3 55.3 %all-to-all-start.1 = ((bf16[8,1024,128]{2,1,0:T(8,128)(2,1)}), bf16[8,1024,128]{2,1,0:T(8,128)(2,1)S(1)}, u32[]{:S(2)}, u32[]{:S(2)}) async-start(bf16[8,1024,128]{2,1,0:T(8,128)(2,1)} %get-tuple-element.24), calls=%async_computation.1 | async-start | bytes 4194304 | tf_op jit(solution)/shard_map/all_to_all | solution.py:435
  40.6 2.0 %collective-permute-start = (bf16[1024,256]{1,0:T(8,128)(2,1)S(1)}, bf16[1024,256]{1,0:T(8,128)(2,1)S(1)}, u32[]{:S(2)}, u32[]{:S(2)}) collective-permute-start(bf16[1024,256]{1,0:T(8,128)(2,1)S(1)} %get-tuple-element.31), channel_id=1, source_target_pairs={{0,1},{1,0},{2,3},{3,2},{4,5},{5,4},{6,7},{7,6},{8,9},{9,8},{10,11... | collective-permute-start | bytes 1572872 | tf_op jit(solution)/shard_map/ocean_sums/ppermute | solution.py:388
  42.7 8.4 %collective-permute-start.1 = (bf16[512,256]{1,0:T(8,128)(2,1)S(1)}, bf16[512,256]{1,0:T(8,128)(2,1)S(1)}, u32[]{:S(2)}, u32[]{:S(2)}) collective-permute-start(bf16[512,256]{1,0:T(8,128)(2,1)S(1)} %get-tuple-element.33), channel_id=1, source_target_pairs={{0,2},{1,3},{2,0},{3,1},{4,6},{5,7},{6,4},{7,5},{8,10},{9,11},{10,... | collective-permute-start | bytes 786440 | tf_op jit(solution)/shard_map/ocean_sums/ppermute | solution.py:388
  51.2 7.5 %collective-permute-start.2 = (bf16[256,256]{1,0:T(8,128)(2,1)S(1)}, bf16[256,256]{1,0:T(8,128)(2,1)S(1)}, u32[]{:S(2)}, u32[]{:S(2)}) collective-permute-start(bf16[256,256]{1,0:T(8,128)(2,1)S(1)} %get-tuple-element.35), channel_id=1, source_target_pairs={{0,4},{4,0},{8,12},{12,8},{16,20},{20,16},{24,28},{28,24},{1,5},{5... | collective-permute-start | bytes 393224 | tf_op jit(solution)/shard_map/ocean_sums/ppermute | solution.py:388
  58.7 14.5 %collective-permute-start.3 = (bf16[64,256]{1,0:T(8,128)(2,1)S(1)}, bf16[64,256]{1,0:T(8,128)(2,1)S(1)}, u32[]{:S(2)}, u32[]{:S(2)}) collective-permute-start(bf16[64,256]{1,0:T(8,128)(2,1)S(1)} %get-tuple-element.37), channel_id=1, source_target_pairs={{0,16},{4,20},{8,24},{12,28},{16,0},{20,4},{24,8},{28,12},{1,17},{... | collective-permute-start | bytes 98312 | tf_op jit(solution)/shard_map/ocean_sums/ppermute | solution.py:388
  61.1 12.1 %collective-permute-start.4 = (bf16[64,256]{1,0:T(8,128)(2,1)S(1)}, bf16[64,256]{1,0:T(8,128)(2,1)S(1)}, u32[]{:S(2)}, u32[]{:S(2)}) collective-permute-start(bf16[64,256]{1,0:T(8,128)(2,1)S(1)} %get-tuple-element.38), channel_id=1, source_target_pairs={{0,8},{4,12},{8,0},{12,4},{16,24},{20,28},{24,16},{28,20},{1,9},{5... | collective-permute-start | bytes 98312 | tf_op jit(solution)/shard_map/ocean_sums/ppermute | solution.py:388
  62.6 10.6 %collective-permute-start.5 = (bf16[64,256]{1,0:T(8,128)(2,1)S(1)}, bf16[64,256]{1,0:T(8,128)(2,1)S(1)}, u32[]{:S(2)}, u32[]{:S(2)}) collective-permute-start(bf16[64,256]{1,0:T(8,128)(2,1)S(1)} %get-tuple-element.39), channel_id=1, source_target_pairs={{0,24},{4,28},{8,16},{12,20},{16,8},{20,12},{24,0},{28,4},{1,25},{... | collective-permute-start | bytes 98312 | tf_op jit(solution)/shard_map/ocean_sums/ppermute | solution.py:388
